TPU v7x, 512 devices: a whole 4x8x8 slice. The times are simulated.
512 devices in a mesh: nodes: 256 (over z, y, x), heads: 2 (over core).
Axes of the slice: x: 4, y: 8, z: 8, core: 2. Of those that a mesh axis runs over, the one named last changes fastest.
Arguments:
- features: bfloat16 [196608, 512], P(('nodes', 'heads')), may hold values from -24 to 24
- w_qkv: bfloat16 [512, 3, 512], replicated, may hold values from -0.25 to 0.25
- w_out: bfloat16 [512, 512], replicated, may hold values from -0.25 to 0.25
- w_up: bfloat16 [512, 1024], replicated, may hold values from -0.25 to 0.25
- w_down: bfloat16 [1024, 512], replicated, may hold values from -0.1875 to 0.1875
- pattern: int32 [1536, 128, 8], P(('nodes', 'heads')), may hold values from 0 to 65535
- partner: int32 [1536, 4], P(('nodes', 'heads')), may hold values from 0 to 2, as said below
- counts: int32 [512], P(('nodes', 'heads')), may hold values from 1 to 3, as said below
Outputs:
- mixed: bfloat16 [196608, 512], P(('nodes', 'heads'))
Inputs may be any that keep to these rules, and one draw needn't show every extreme that they name: `partner`: each link of block slot s of device d names a live block slot of device d XOR 2**b_l; every live slot of that device is named by some slot of d. `counts`: some device holds 3 live blocks.
All inputs are finite; a program needn't handle non-finite values.
Results may differ from a plain program's by a relative error of at most 0.012.
The roundings to bfloat16 on the way count: a program that leaves them out, or rounds other values in their place, can miss the bound.
Values may be sent and summed in bfloat16 or wider, within the bound.
No kernel may reach another device: no remote copies, remote signals or barrier semaphores. Data moves between devices by JAX's collectives and lax.ppermute only.
A program may use at most 64 MiB of HBM per device.

v0:
```python
import jax
import jax.numpy as jnp
from jax import lax
from jax.sharding import PartitionSpec as P

D = 512
H = 8


epsilon = 1e-05


def from_partner(value, axis, bit):
    mask = 2**bit
    pairs = [(source, source ^ mask) for source in range(lax.axis_size(axis))]
    return lax.ppermute(value, axis, pairs)


def unpack_bits(pattern_words, width):
    column = jnp.arange(width)
    picked = pattern_words[..., column // 16]
    bits = jnp.right_shift(picked, column % 16) & 1
    return (bits == 1) | jnp.eye(width, dtype=bool)


def local(features, w_qkv, w_out, w_up, w_down, pattern, partner, counts):
    row_count = features.shape[0]
    slot_count = partner.shape[0]
    block_rows = row_count // slot_count
    width = features.shape[1]
    head_size = D // H
    projected = jnp.einsum(
        "rd,dtc->rtc", features, w_qkv, preferred_element_type=jnp.float32
    ).astype(jnp.bfloat16)
    keys_values = projected[:, 1:, :]
    log_size = (lax.axis_size("nodes") * lax.axis_size("heads")).bit_length() - 1
    linked_parts = []
    for link_index in range(4):
        bit_place = link_index * log_size // 4
        if bit_place == 0:
            received = from_partner(keys_values, "heads", 0)
        else:
            received = from_partner(keys_values, "nodes", bit_place - 1)
        received = received.reshape(slot_count, block_rows, 2, width)
        linked_parts.append(jnp.take(received, partner[:, link_index], axis=0))
    own_blocks = projected.reshape(slot_count, block_rows, 3, width)
    all_keys = jnp.concatenate([own_blocks[:, :, 1:]] + linked_parts, axis=1)
    local_allowed = unpack_bits(pattern, block_rows)
    allowed = jnp.concatenate(
        [local_allowed, jnp.ones((slot_count, block_rows, 4 * block_rows), dtype=bool)], axis=2
    )
    score_scale = 1.0 / head_size**0.5
    head_outputs = []
    for head_index in range(H):
        lower = head_index * head_size
        queries = own_blocks[:, :, 0, lower : lower + head_size]
        keys = all_keys[:, :, 0, lower : lower + head_size]
        values = all_keys[:, :, 1, lower : lower + head_size]
        scores = (
            jnp.einsum("sqe,ske->sqk", queries, keys, preferred_element_type=jnp.float32)
            * score_scale
        )
        scores = jnp.where(allowed, scores, -1e30)
        top_score = jnp.max(scores, axis=-1, keepdims=True)
        expo = jnp.exp(scores - top_score)
        weights = (expo / jnp.sum(expo, axis=-1, keepdims=True)).astype(jnp.bfloat16)
        result = jnp.einsum("sqk,ske->sqe", weights, values, preferred_element_type=jnp.float32)
        head_outputs.append(result.astype(jnp.bfloat16))
    attended = jnp.concatenate(head_outputs, axis=-1).reshape(row_count, width)
    resid = features.astype(jnp.float32) + jnp.dot(
        attended, w_out, preferred_element_type=jnp.float32
    )
    row_mean = jnp.mean(resid, axis=1, keepdims=True)
    row_var = jnp.mean(resid * resid, axis=1, keepdims=True) - row_mean * row_mean
    normed = (resid - row_mean) * lax.rsqrt(row_var + epsilon)
    hidden = jax.nn.relu(
        jnp.dot(normed.astype(jnp.bfloat16), w_up, preferred_element_type=jnp.float32)
    ).astype(jnp.bfloat16)
    ffn = jnp.dot(hidden, w_down, preferred_element_type=jnp.float32)
    mixed = normed + ffn
    live_rows = jnp.arange(row_count) // block_rows < counts[0]
    return jnp.where(live_rows[:, None], mixed, 0.0).astype(jnp.bfloat16)


def solution(mesh):
    placed = (
        P(("nodes", "heads"), None),
        P(),
        P(),
        P(),
        P(),
        P(("nodes", "heads"), None, None),
        P(("nodes", "heads"), None),
        P(("nodes", "heads")),
    )
    return jax.shard_map(
        local, mesh=mesh, in_specs=placed, out_specs=P(("nodes", "heads"), None), check_vma=False
    )
```

profile of v0, /device:TPU:1, one launch (start us, length us, event | category | flops | bytes accessed | tf_op | source)
XLA Modules:
  0.0 129.7 jit_solution(13987496136526952900)
XLA Ops:
  4.1 8.8 %collective-permute-start = (bf16[384,2,512]{2,0,1:T(8,128)(2,1)}, bf16[384,2,512]{2,0,1:T(8,128)(2,1)}, u32[]{:S(2)}, u32[]{:S(2)}) collective-permute-start(bf16[384,2,512]{2,0,1:T(8,128)(2,1)} %slice.132), channel_id=1, source_target_pairs={{0,1},{1,0},{2,3},{3,2},{4,5},{5,4},{6,7},{7,6},{8,9},{9,8},{10,11... | collective-permute-start | bytes 2359304 | tf_op jit(solution)/shard_map/ppermute | solution.py:16
  16.8 3.7 %collective-permute-start.3 = (bf16[384,2,512]{2,0,1:T(8,128)(2,1)}, bf16[384,2,512]{2,0,1:T(8,128)(2,1)}, u32[]{:S(2)}, u32[]{:S(2)}) collective-permute-start(bf16[384,2,512]{2,0,1:T(8,128)(2,1)} %slice.132), channel_id=1, source_target_pairs={{0,64},{2,66},{4,68},{6,70},{8,72},{10,74},{12,76},{14,78},{16,80}... | collective-permute-start | bytes 2359304 | tf_op jit(solution)/shard_map/ppermute | solution.py:16
  29.0 2.2 %copy.21 = bf16[3,128,2,512]{3,1,2,0:T(8,128)(2,1)} copy(bf16[3,128,2,512]{3,1,0,2:T(8,128)(2,1)} %bitcast.6) | data formatting | bytes 1572864 | tf_op jit(solution)/shard_map/reshape | solution.py:44
  31.2 2.7 %gather_fusion.1 = bf16[3,128,2,512]{3,1,2,0:T(8,128)(2,1)} fusion(bf16[3,128,2,512]{3,1,2,0:T(8,128)(2,1)} %copy.21, s32[1024]{0:T(1024)S(1)} %pad_clamp_fusion.3), kind=kCustom, calls=%fused_computation.clone | custom fusion | bytes 1572876 | tf_op jit(solution)/shard_map/jit(_take)/gather | solution.py:45
  33.9 2.3 %copy.22 = bf16[3,128,2,512]{1,3,0,2:T(8,128)(2,1)} copy(bf16[3,128,2,512]{3,1,2,0:T(8,128)(2,1)} %gather_fusion.1) | data formatting | bytes 1572864 | tf_op jit(solution)/shard_map/jit(_take)/gather | solution.py:45
  38.4 2.7 %gather_fusion.2 = bf16[3,128,2,512]{3,1,2,0:T(8,128)(2,1)} fusion(bf16[3,128,2,512]{3,1,2,0:T(8,128)(2,1)} %copy.23, s32[1024]{0:T(1024)S(1)} %pad_clamp_fusion.2), kind=kCustom, calls=%fused_computation.1.clone | custom fusion | bytes 1572876 | tf_op jit(solution)/shard_map/jit(_take)/gather | solution.py:45
  41.1 2.3 %copy.24 = bf16[3,128,2,512]{1,3,0,2:T(8,128)(2,1)} copy(bf16[3,128,2,512]{3,1,2,0:T(8,128)(2,1)} %gather_fusion.2) | data formatting | bytes 1572864 | tf_op jit(solution)/shard_map/jit(_take)/gather | solution.py:45
  43.4 9.3 %collective-permute-done.2 = bf16[384,2,512]{2,0,1:T(8,128)(2,1)} collective-permute-done((bf16[384,2,512]{2,0,1:T(8,128)(2,1)}, bf16[384,2,512]{2,0,1:T(8,128)(2,1)}, u32[]{:S(2)}, u32[]{:S(2)}) %collective-permute-start.2) | collective-permute-done | bytes 786464 | tf_op jit(solution)/shard_map/ppermute | solution.py:16
  54.9 2.7 %gather_fusion.3 = bf16[3,128,2,512]{3,1,2,0:T(8,128)(2,1)} fusion(bf16[3,128,2,512]{3,1,2,0:T(8,128)(2,1)} %copy.25, s32[1024]{0:T(1024)S(1)} %pad_clamp_fusion.1), kind=kCustom, calls=%fused_computation.2.clone | custom fusion | bytes 1572876 | tf_op jit(solution)/shard_map/jit(_take)/gather | solution.py:45
  57.6 2.3 %copy.26 = bf16[3,128,2,512]{1,3,0,2:T(8,128)(2,1)} copy(bf16[3,128,2,512]{3,1,2,0:T(8,128)(2,1)} %gather_fusion.3) | data formatting | bytes 1572864 | tf_op jit(solution)/shard_map/jit(_take)/gather | solution.py:45
  62.0 2.6 %gather_fusion.4 = bf16[3,128,2,512]{3,1,2,0:T(8,128)(2,1)} fusion(bf16[3,128,2,512]{3,1,2,0:T(8,128)(2,1)} %copy.27, s32[1024]{0:T(1024)S(1)} %pad_clamp_fusion), kind=kCustom, calls=%fused_computation.3.clone | custom fusion | bytes 1572876 | tf_op jit(solution)/shard_map/jit(_take)/gather | solution.py:45
  64.7 2.3 %copy.28 = bf16[3,128,2,512]{1,3,0,2:T(8,128)(2,1)} copy(bf16[3,128,2,512]{3,1,2,0:T(8,128)(2,1)} %gather_fusion.4) | data formatting | bytes 1572864 | tf_op jit(solution)/shard_map/jit(_take)/gather | solution.py:45
  67.0 2.4 %select_dynamic-update-slice_fusion.3 = bf16[3,640,2,512]{1,3,0,2:T(8,128)(2,1)} fusion(bf16[3,640,2,512]{1,3,0,2:T(8,128)(2,1)} %constant_dynamic-update-slice_fusion, bf16[3,128,2,512]{1,3,0,2:T(8,128)(2,1)} %copy.22, pred[3]{0:T(512)(128)(4,1)S(1)} %get-tuple-element.18), kind=kLoop, calls=%fused_computation.79 | loop fusion | flops 393216 | bytes 1572867
  69.3 2.4 %select_dynamic-update-slice_fusion.2 = bf16[3,640,2,512]{1,3,0,2:T(8,128)(2,1)} fusion(bf16[3,640,2,512]{1,3,0,2:T(8,128)(2,1)} %select_dynamic-update-slice_fusion.3, bf16[3,128,2,512]{1,3,0,2:T(8,128)(2,1)} %copy.24, pred[3]{0:T(512)(128)(4,1)S(1)} %get-tuple-element.17), kind=kLoop, calls=%fused_computation.78 | loop fusion | flops 393216 | bytes 1572867
  71.7 2.3 %select_dynamic-update-slice_fusion.1 = bf16[3,640,2,512]{1,3,0,2:T(8,128)(2,1)} fusion(bf16[3,640,2,512]{1,3,0,2:T(8,128)(2,1)} %select_dynamic-update-slice_fusion.2, bf16[3,128,2,512]{1,3,0,2:T(8,128)(2,1)} %copy.26, pred[3]{0:T(512)(128)(4,1)S(1)} %get-tuple-element.16), kind=kLoop, calls=%fused_computation.77 | loop fusion | flops 393216 | bytes 1572867
  75.2 2.2 %pad_select_fusion.6 = f32[3,128,640]{2,1,0:T(8,128)} fusion(pred[3,128,128]{2,1,0:T(32,128)(4,1)S(1)} %fusion.46, bf16[3,640,2,512]{1,3,0,2:T(8,128)(2,1)} %select_dynamic-update-slice_fusion, bf16[3,128,3,512]{3,1,0,2:T(8,128)(2,1)S(1)} %bitcast.175), kind=kOutput, calls=%fused_computation.19 | convolution fusion | flops 31948800 | bytes 1376256 | tf_op jit(solution)/shard_map/sqe,ske->sqk/dot_general | solution.py:60
  78.9 2.2 %pad_select_fusion.7 = f32[3,128,640]{2,1,0:T(8,128)} fusion(pred[3,128,128]{2,1,0:T(32,128)(4,1)S(1)} %fusion.46, bf16[3,640,2,512]{1,3,0,2:T(8,128)(2,1)} %select_dynamic-update-slice_fusion, bf16[3,128,3,512]{3,1,0,2:T(8,128)(2,1)S(1)} %bitcast.177), kind=kOutput, calls=%fused_computation.20 | convolution fusion | flops 31948800 | bytes 1376256 | tf_op jit(solution)/shard_map/sqe,ske->sqk/dot_general | solution.py:60
  82.5 2.2 %pad_select_fusion.5 = f32[3,128,640]{2,1,0:T(8,128)} fusion(pred[3,128,128]{2,1,0:T(32,128)(4,1)S(1)} %fusion.46, bf16[3,640,2,512]{1,3,0,2:T(8,128)(2,1)} %select_dynamic-update-slice_fusion, bf16[3,128,3,512]{3,1,0,2:T(8,128)(2,1)S(1)} %bitcast.179), kind=kOutput, calls=%fused_computation.18 | convolution fusion | flops 31948800 | bytes 1376256 | tf_op jit(solution)/shard_map/sqe,ske->sqk/dot_general | solution.py:60
  86.2 2.2 %pad_select_fusion.4 = f32[3,128,640]{2,1,0:T(8,128)} fusion(pred[3,128,128]{2,1,0:T(32,128)(4,1)S(1)} %fusion.46, bf16[3,640,2,512]{1,3,0,2:T(8,128)(2,1)} %select_dynamic-update-slice_fusion, bf16[3,128,3,512]{3,1,0,2:T(8,128)(2,1)S(1)} %bitcast.181), kind=kOutput, calls=%fused_computation.17 | convolution fusion | flops 31948800 | bytes 1376256 | tf_op jit(solution)/shard_map/sqe,ske->sqk/dot_general | solution.py:60
  89.9 2.3 %pad_select_fusion.3 = f32[3,128,640]{2,1,0:T(8,128)} fusion(pred[3,128,128]{2,1,0:T(32,128)(4,1)S(1)} %fusion.46, bf16[3,640,2,512]{1,3,0,2:T(8,128)(2,1)} %select_dynamic-update-slice_fusion, bf16[3,128,3,512]{3,1,0,2:T(8,128)(2,1)S(1)} %bitcast.183), kind=kOutput, calls=%fused_computation.16 | convolution fusion | flops 31948800 | bytes 1376256 | tf_op jit(solution)/shard_map/sqe,ske->sqk/dot_general | solution.py:60
  93.6 2.3 %pad_select_fusion.2 = f32[3,128,640]{2,1,0:T(8,128)} fusion(pred[3,128,128]{2,1,0:T(32,128)(4,1)S(1)} %fusion.46, bf16[3,640,2,512]{1,3,0,2:T(8,128)(2,1)} %select_dynamic-update-slice_fusion, bf16[3,128,3,512]{3,1,0,2:T(8,128)(2,1)S(1)} %bitcast.185), kind=kOutput, calls=%fused_computation.15 | convolution fusion | flops 31948800 | bytes 1376256 | tf_op jit(solution)/shard_map/sqe,ske->sqk/dot_general | solution.py:60
  97.4 2.2 %pad_select_fusion.1 = f32[3,128,640]{2,1,0:T(8,128)} fusion(pred[3,128,128]{2,1,0:T(32,128)(4,1)S(1)} %fusion.46, bf16[3,640,2,512]{1,3,0,2:T(8,128)(2,1)} %select_dynamic-update-slice_fusion, bf16[3,128,3,512]{3,1,0,2:T(8,128)(2,1)S(1)} %bitcast.187), kind=kOutput, calls=%fused_computation.14 | convolution fusion | flops 31948800 | bytes 1376256 | tf_op jit(solution)/shard_map/sqe,ske->sqk/dot_general | solution.py:60
  101.1 2.3 %pad_select_fusion = f32[3,128,640]{2,1,0:T(8,128)} fusion(pred[3,128,128]{2,1,0:T(32,128)(4,1)S(1)} %fusion.46, bf16[3,640,2,512]{1,3,0,2:T(8,128)(2,1)} %select_dynamic-update-slice_fusion, bf16[3,128,3,512]{3,1,0,2:T(8,128)(2,1)S(1)} %bitcast.189), kind=kOutput, calls=%fused_computation.13 | convolution fusion | flops 31948800 | bytes 1376256 | tf_op jit(solution)/shard_map/sqe,ske->sqk/dot_general | solution.py:60
  104.8 2.4 %fusion.35 = bf16[3,128,512]{1,2,0:T(8,128)(2,1)S(1)} fusion(f32[3,128]{1,0:T(4,128)S(1)} %fusion.86, bf16[3,640,2,512]{1,3,0,2:T(8,128)(2,1)} %select_dynamic-update-slice_fusion, f32[3,128,640]{2,1,0:T(8,128)} %pad_select_fusion.7), kind=kOutput, calls=%fused_computation.67 | convolution fusion | flops 32220158 | bytes 2262528 | tf_op jit(solution)/shard_map/sqk,ske->sqe/dot_general | solution.py:67
  107.2 2.4 %fusion.34 = bf16[3,128,512]{1,2,0:T(8,128)(2,1)S(1)} fusion(bf16[3,128,512]{1,2,0:T(8,128)(2,1)S(1)} %fusion.35, f32[3,128]{1,0:T(4,128)S(1)} %fusion.87, bf16[3,640,2,512]{1,3,0,2:T(8,128)(2,1)} %select_dynamic-update-slice_fusion, f32[3,128,640]{2,1,0:T(8,128)} %pad_select_fusion.6), kind=kOutput, calls=%fused_computation.65 | convolution fusion | flops 32220160 | bytes 2263040 | tf_op jit(solution)/shard_map/sqk,ske->sqe/dot_general | solution.py:67
  109.7 2.4 %fusion.33 = bf16[3,128,512]{1,2,0:T(8,128)(2,1)S(1)} fusion(bf16[3,128,512]{1,2,0:T(8,128)(2,1)S(1)} %fusion.34, f32[3,128]{1,0:T(4,128)S(1)} %fusion.88, bf16[3,640,2,512]{1,3,0,2:T(8,128)(2,1)} %select_dynamic-update-slice_fusion, f32[3,128,640]{2,1,0:T(8,128)} %pad_select_fusion.5), kind=kOutput, calls=%fused_computation.63 | convolution fusion | flops 32220160 | bytes 2263040 | tf_op jit(solution)/shard_map/sqk,ske->sqe/dot_general | solution.py:67
  112.1 2.4 %fusion.32 = bf16[3,128,512]{1,2,0:T(8,128)(2,1)S(1)} fusion(bf16[3,128,512]{1,2,0:T(8,128)(2,1)S(1)} %fusion.33, f32[3,128]{1,0:T(4,128)S(1)} %fusion.89, bf16[3,640,2,512]{1,3,0,2:T(8,128)(2,1)} %select_dynamic-update-slice_fusion, f32[3,128,640]{2,1,0:T(8,128)} %pad_select_fusion.4), kind=kOutput, calls=%fused_computation.61 | convolution fusion | flops 32220160 | bytes 2263040 | tf_op jit(solution)/shard_map/sqk,ske->sqe/dot_general | solution.py:67
  114.5 2.6 %fusion.31 = bf16[3,128,512]{1,2,0:T(8,128)(2,1)S(1)} fusion(bf16[3,128,512]{1,2,0:T(8,128)(2,1)S(1)} %fusion.32, f32[3,128]{1,0:T(4,128)S(1)} %fusion.90, bf16[3,640,2,512]{1,3,0,2:T(8,128)(2,1)} %select_dynamic-update-slice_fusion, f32[3,128,640]{2,1,0:T(8,128)} %pad_select_fusion.3), kind=kOutput, calls=%fused_computation.59 | convolution fusion | flops 32220160 | bytes 2263040 | tf_op jit(solution)/shard_map/sqk,ske->sqe/dot_general | solution.py:67
  117.1 2.7 %fusion.30 = bf16[3,128,512]{1,2,0:T(8,128)(2,1)S(1)} fusion(bf16[3,128,512]{1,2,0:T(8,128)(2,1)S(1)} %fusion.31, f32[3,128]{1,0:T(4,128)S(1)} %fusion.91, bf16[3,640,2,512]{1,3,0,2:T(8,128)(2,1)} %select_dynamic-update-slice_fusion, f32[3,128,640]{2,1,0:T(8,128)} %pad_select_fusion.2), kind=kOutput, calls=%fused_computation.57 | convolution fusion | flops 32220160 | bytes 2263040 | tf_op jit(solution)/shard_map/sqk,ske->sqe/dot_general | solution.py:67
  119.8 2.4 %fusion.29 = bf16[3,128,512]{1,2,0:T(8,128)(2,1)S(1)} fusion(bf16[3,128,512]{1,2,0:T(8,128)(2,1)S(1)} %fusion.30, f32[3,128]{1,0:T(4,128)S(1)} %fusion.92, bf16[3,640,2,512]{1,3,0,2:T(8,128)(2,1)} %select_dynamic-update-slice_fusion, f32[3,128,640]{2,1,0:T(8,128)} %pad_select_fusion.1), kind=kOutput, calls=%fused_computation.55 | convolution fusion | flops 32220160 | bytes 2263040 | tf_op jit(solution)/shard_map/sqk,ske->sqe/dot_general | solution.py:67
  122.2 2.4 %fusion.28 = bf16[3,128,512]{1,2,0:T(8,128)(2,1)S(1)} fusion(bf16[3,128,512]{1,2,0:T(8,128)(2,1)S(1)} %fusion.29, f32[3,128]{1,0:T(4,128)S(1)} %fusion.93, bf16[3,640,2,512]{1,3,0,2:T(8,128)(2,1)} %select_dynamic-update-slice_fusion, f32[3,128,640]{2,1,0:T(8,128)} %pad_select_fusion), kind=kOutput, calls=%fused_computation.53 | convolution fusion | flops 32220160 | bytes 2263040 | tf_op jit(solution)/shard_map/sqk,ske->sqe/dot_general | solution.py:67
  126.3 3.3 %fusion.27 = bf16[384,512]{1,0:T(8,128)(2,1)} fusion(bf16[1024,512]{1,0:T(8,128)(2,1)} %param.14, bf16[512,1024]{1,0:T(8,128)(2,1)} %param.13, f32[384,512]{1,0:T(8,128)S(1)} %get-tuple-element.14, f32[384]{0:T(512)S(1)} %get-tuple-element.13, f32[384]{0:T(512)S(1)} %get-tuple-element.12, pred[384]{0:T(512)(128)(4,1)S(1)} %fusion.55), kind=kOutput, calls=%fused_computation.51 | convolution fusion | flops 807665664 | bytes 3280256 | tf_op jit(solution)/shard_map/dot_general | solution.py:79
  (54 shorter events, 36.9 us)
Async XLA Ops:
  0.0 1.4 %copy-start = (bf16[512,3,512]{2,0,1:T(8,128)(2,1)S(1)}, bf16[512,3,512]{2,0,1:T(8,128)(2,1)}, u32[]{:S(2)}) copy-start(bf16[512,3,512]{2,0,1:T(8,128)(2,1)} %param.11) | copy-start | bytes 4718596
  3.2 22.4 %copy-start.4 = (s32[3,4]{1,0:T(4,128)S(1)}, s32[3,4]{1,0:T(4,128)}, u32[]{:S(2)}) copy-start(s32[3,4]{1,0:T(4,128)} %param.16) | copy-start | bytes 148
  3.2 23.4 %copy-start.1 = (s32[3,128,8]{1,2,0:T(8,128)S(1)}, s32[3,128,8]{1,2,0:T(8,128)}, u32[]{:S(2)}) copy-start(s32[3,128,8]{1,2,0:T(8,128)} %param.15) | copy-start | bytes 36868
  4.1 24.9 %collective-permute-start = (bf16[384,2,512]{2,0,1:T(8,128)(2,1)}, bf16[384,2,512]{2,0,1:T(8,128)(2,1)}, u32[]{:S(2)}, u32[]{:S(2)}) collective-permute-start(bf16[384,2,512]{2,0,1:T(8,128)(2,1)} %slice.132), channel_id=1, source_target_pairs={{0,1},{1,0},{2,3},{3,2},{4,5},{5,4},{6,7},{7,6},{8,9},{9,8},{10,11... | collective-permute-start | bytes 2359304 | tf_op jit(solution)/shard_map/ppermute | solution.py:16
  12.9 23.3 %collective-permute-start.1 = (bf16[384,2,512]{2,0,1:T(8,128)(2,1)}, bf16[384,2,512]{2,0,1:T(8,128)(2,1)}, u32[]{:S(2)}, u32[]{:S(2)}) collective-permute-start(bf16[384,2,512]{2,0,1:T(8,128)(2,1)} %slice.132), channel_id=1, source_target_pairs={{0,4},{2,6},{4,0},{6,2},{8,12},{10,14},{12,8},{14,10},{16,20},{18,... | collective-permute-start | bytes 2359304 | tf_op jit(solution)/shard_map/ppermute | solution.py:16
  14.9 37.9 %collective-permute-start.2 = (bf16[384,2,512]{2,0,1:T(8,128)(2,1)}, bf16[384,2,512]{2,0,1:T(8,128)(2,1)}, u32[]{:S(2)}, u32[]{:S(2)}) collective-permute-start(bf16[384,2,512]{2,0,1:T(8,128)(2,1)} %slice.132), channel_id=1, source_target_pairs={{0,16},{2,18},{4,20},{6,22},{8,24},{10,26},{12,28},{14,30},{16,0},... | collective-permute-start | bytes 2359304 | tf_op jit(solution)/shard_map/ppermute | solution.py:16
  16.8 43.1 %collective-permute-start.3 = (bf16[384,2,512]{2,0,1:T(8,128)(2,1)}, bf16[384,2,512]{2,0,1:T(8,128)(2,1)}, u32[]{:S(2)}, u32[]{:S(2)}) collective-permute-start(bf16[384,2,512]{2,0,1:T(8,128)(2,1)} %slice.132), channel_id=1, source_target_pairs={{0,64},{2,66},{4,68},{6,70},{8,72},{10,74},{12,76},{14,78},{16,80}... | collective-permute-start | bytes 2359304 | tf_op jit(solution)/shard_map/ppermute | solution.py:16
  67.0 7.0 %copy-start.2 = (bf16[3,128,2,512]{1,3,0,2:T(8,128)(2,1)S(1)}, bf16[3,128,2,512]{1,3,0,2:T(8,128)(2,1)}, u32[]{:S(2)}) copy-start(bf16[3,128,2,512]{1,3,0,2:T(8,128)(2,1)} %copy.28) | copy-start | bytes 2359300
  119.8 5.0 %copy-start.3 = (bf16[512,512]{1,0:T(8,128)(2,1)S(1)}, bf16[512,512]{1,0:T(8,128)(2,1)}, u32[]{:S(2)}) copy-start(bf16[512,512]{1,0:T(8,128)(2,1)} %param.12) | copy-start | bytes 1572868
where the time goes:
time: 131 us; the launch traced here: 130 us
  matrix products  56 us (43%)
  local copies, waits for them, and re-layouts  35.8 us (27%)
  starting transfers between devices  16.3 us (12%)
  other arithmetic  11.4 us (9%)
  waiting for transfers between devices  9.33 us (7%)
    gather x8, local copies, waits for them, and re-layouts, local(): linked_parts.append(jnp.take(received, partner[:, link_index], axis=0))  20 us
    dot_general x8, matrix products, local(): jnp.einsum('sqk,ske->sqe', weights, values, preferred_element_type=jnp.fl...  19.8 us
    dot_general x8, matrix products, local(): jnp.einsum('sqe,ske->sqk', queries, keys, preferred_element_type=jnp.floa...  17.9 us
    ppermute x4, starting transfers between devices, from_partner(): return lax.ppermute(value, axis, pairs)  16.3 us
    sub x8, matrix products, local(): expo = jnp.exp(scores - top_score)  11.8 us
    ppermute x4, waiting for transfers between devices, from_partner(): return lax.ppermute(value, axis, pairs)  9.33 us
    reshape x4, local copies, waits for them, and re-layouts, local(): received = received.reshape(slot_count, block_rows, 2, width)  8.56 us
    unnamed x3, other arithmetic  7.02 us
  transfers between devices with their start and end apart: 4, of which 1 were waited for; matrix products, arithmetic and copies ran while one was open for 23% of the time, Pallas kernels for 0%

commit v1 on v0

v1 whole, which is shorter than its diff:
```python
import jax
import jax.numpy as jnp
from jax import lax
from jax.experimental import pallas as pl
from jax.experimental.pallas import tpu as pltpu
from jax.sharding import PartitionSpec as P

D = 512
H = 8
HEAD = D // H
BLK = 128
SLOTS = 3
ROWS = SLOTS * BLK
PAIRS = H // 2
EPSILON = 1e-05
SCALE = 1.4426950408889634 / HEAD**0.5
F32 = jnp.float32
BF16 = jnp.bfloat16


def from_partner(value, axis, bit):
    mask = 2**bit
    pairs = [(source, source ^ mask) for source in range(lax.axis_size(axis))]
    return lax.ppermute(value, axis, pairs)


def mm(a, b):
    return jnp.dot(a, b, preferred_element_type=F32)


def low_half(shape):
    return lax.broadcasted_iota(jnp.int32, shape, 1) < HEAD


def split_heads(pair):
    low = low_half(pair.shape)
    zero = jnp.zeros_like(pair)
    return jnp.where(low, pair, zero), jnp.where(low, zero, pair)


def attend(q, k, v, allowed):
    q_low, q_high = split_heads(q)
    scores = lax.dot_general(
        jnp.concatenate([q_low, q_high], axis=0), k, (((1,), (1,)), ((), ())), preferred_element_type=F32
    )
    if allowed is not None:
        scores = jnp.where(allowed, scores, -1e30)
    top = jnp.max(scores, axis=1, keepdims=True)
    weights = jnp.exp2((scores - top) * SCALE).astype(BF16)
    weights = jnp.concatenate([weights[:BLK], weights[BLK:]], axis=1)
    v_low, v_high = split_heads(v)
    one_low, one_high = split_heads(jnp.ones_like(v))
    values = jnp.concatenate(
        [jnp.concatenate([v_low, one_low], axis=1), jnp.concatenate([v_high, one_high], axis=1)], axis=0
    )
    result = mm(weights, values)
    low = low_half((BLK, 2 * HEAD))
    return result[:, : 2 * HEAD], result[:, 2 * HEAD :], jnp.where(low, top[:BLK], top[BLK:])


def merge(first, second):
    o1, l1, m1 = first
    o2, l2, m2 = second
    m = jnp.maximum(m1, m2)
    a = jnp.exp2((m1 - m) * SCALE)
    b = jnp.exp2((m2 - m) * SCALE)
    return o1 * a + o2 * b, l1 * a + l2 * b, m


def local_mask(words):
    word_count = words.shape[0]
    halves = jnp.concatenate([words & 255, jnp.right_shift(words, 8)], axis=0).astype(F32).astype(BF16)
    row = lax.broadcasted_iota(jnp.int32, (2 * word_count, BLK), 0)
    column = lax.broadcasted_iota(jnp.int32, (2 * word_count, BLK), 1)
    source = column // 16 + word_count * (column % 16 // 8)
    pick = jnp.where(row == source, 1.0, 0.0).astype(BF16)
    picked = lax.dot_general(halves, pick, (((0,), (0,)), ((), ())), preferred_element_type=F32)
    query = lax.broadcasted_iota(jnp.int32, (BLK, BLK), 0)
    key = lax.broadcasted_iota(jnp.int32, (BLK, BLK), 1)
    bits = jnp.right_shift(picked.astype(jnp.int32), key % 8) & 1
    return (bits == 1) | (query == key)


def slot_rows(slot):
    return pl.ds(pl.multiple_of(slot * BLK, BLK), BLK)


def pair_columns(pair):
    return slice(pair * 2 * HEAD, (pair + 1) * 2 * HEAD)


def own_kernel(link, partner, x, r, w, words, q_out, o_out, l_out, m_out, k_own, v_own, k_far, v_far):
    q_out[...] = mm(x[...], w[0]).astype(BF16)
    k_own[...] = mm(x[...], w[1]).astype(BF16)
    v_own[...] = mm(x[...], w[2]).astype(BF16)
    k_far[...] = mm(r[...], w[1]).astype(BF16)
    v_far[...] = mm(r[...], w[2]).astype(BF16)
    for s in range(SLOTS):
        rows = slice(s * BLK, (s + 1) * BLK)
        far = slot_rows(partner[s, link])
        mask = local_mask(words[s])
        mask = jnp.concatenate([mask, jnp.ones((BLK, BLK), dtype=jnp.bool_)], axis=1)
        mask = jnp.concatenate([mask, mask], axis=0)
        for p in range(PAIRS):
            cols = pair_columns(p)
            k = jnp.concatenate([k_own[rows, cols], k_far[far, cols]], axis=0)
            v = jnp.concatenate([v_own[rows, cols], v_far[far, cols]], axis=0)
            o, l, m = attend(q_out[rows, cols], k, v, mask)
            o_out[rows, cols] = o
            l_out[rows, cols] = l
            m_out[rows, cols] = m


def far_kernel(link_a, link_b, partner, ra, rb, w, q, o_in, l_in, m_in, o_out, l_out, m_out, ka, va, kb, vb):
    ka[...] = mm(ra[...], w[1]).astype(BF16)
    va[...] = mm(ra[...], w[2]).astype(BF16)
    kb[...] = mm(rb[...], w[1]).astype(BF16)
    vb[...] = mm(rb[...], w[2]).astype(BF16)
    for s in range(SLOTS):
        rows = slice(s * BLK, (s + 1) * BLK)
        far_a = slot_rows(partner[s, link_a])
        far_b = slot_rows(partner[s, link_b])
        for p in range(PAIRS):
            cols = pair_columns(p)
            k = jnp.concatenate([ka[far_a, cols], kb[far_b, cols]], axis=0)
            v = jnp.concatenate([va[far_a, cols], vb[far_b, cols]], axis=0)
            part = attend(q[rows, cols], k, v, None)
            o, l, m = merge((o_in[rows, cols], l_in[rows, cols], m_in[rows, cols]), part)
            o_out[rows, cols] = o
            l_out[rows, cols] = l
            m_out[rows, cols] = m


def last_kernel(link, partner, counts, r, w, q, o_in, l_in, m_in, x, w_out, w_up, w_down, out, k_far, v_far, att):
    k_far[...] = mm(r[...], w[1]).astype(BF16)
    v_far[...] = mm(r[...], w[2]).astype(BF16)
    for s in range(SLOTS):
        rows = slice(s * BLK, (s + 1) * BLK)
        far = slot_rows(partner[s, link])
        for p in range(PAIRS):
            cols = pair_columns(p)
            part = attend(q[rows, cols], k_far[far, cols], v_far[far, cols], None)
            o, l, _ = merge((o_in[rows, cols], l_in[rows, cols], m_in[rows, cols]), part)
            att[rows, cols] = (o / l).astype(BF16)
    resid = x[...].astype(F32) + mm(att[...], w_out[...])
    mean = jnp.mean(resid, axis=1, keepdims=True)
    var = jnp.mean(resid * resid, axis=1, keepdims=True) - mean * mean
    normed = (resid - mean) * lax.rsqrt(var + EPSILON)
    hidden = jnp.maximum(mm(normed.astype(BF16), w_up[...]), 0.0).astype(BF16)
    mixed = normed + mm(hidden, w_down[...])
    slot = lax.broadcasted_iota(jnp.int32, (ROWS, 1), 0) // BLK
    out[...] = jnp.where(slot < counts[0], mixed, 0.0).astype(BF16)


VMEM = pl.BlockSpec(memory_space=pltpu.VMEM)
SMEM = pl.BlockSpec(memory_space=pltpu.SMEM)


def wide(dtype):
    return jax.ShapeDtypeStruct((ROWS, D), dtype)


def scratch(n):
    return [pltpu.VMEM((ROWS, D), BF16) for _ in range(n)]


def call(kernel, smem, vmem, outs, n_scratch, flops, name):
    return pl.pallas_call(
        kernel,
        out_shape=outs,
        in_specs=[SMEM] * len(smem) + [VMEM] * len(vmem),
        out_specs=jax.tree.map(lambda _: VMEM, outs),
        scratch_shapes=scratch(n_scratch),
        compiler_params=pltpu.CompilerParams(vmem_limit_bytes=24 * 2**20),
        cost_estimate=pl.CostEstimate(flops=flops, bytes_accessed=4 * 2**20, transcendentals=0),
        name=name,
    )(*smem, *vmem)


def local(features, w_qkv, w_out, w_up, w_down, pattern, partner, counts):
    log_size = (lax.axis_size("nodes") * lax.axis_size("heads")).bit_length() - 1
    bits = [link * log_size // 4 for link in range(4)]
    received = {}
    for link in (2, 1, 3, 0):
        bit = bits[link]
        received[link] = (
            from_partner(features, "heads", 0) if bit == 0 else from_partner(features, "nodes", bit - 1)
        )
    w = jnp.transpose(w_qkv, (1, 0, 2))
    words = jnp.transpose(pattern, (0, 2, 1))
    state = [wide(F32)] * 3
    q, *parts = call(
        lambda *refs: own_kernel(0, *refs),
        [partner], [features, received[0], w, words], [wide(BF16)] + state, 4, 2 * 10**9, "own_and_core",
    )
    parts = call(
        lambda *refs: far_kernel(1, 3, *refs),
        [partner], [received[1], received[3], w, q, *parts], state, 4, 2 * 10**9, "far_x_z",
    )
    return call(
        lambda *refs: last_kernel(2, *refs),
        [partner, counts], [received[2], w, q, *parts, features, w_out, w_up, w_down], wide(BF16), 3, 2 * 10**9, "far_y_mix",
    )


def solution(mesh):
    placed = (
        P(("nodes", "heads"), None),
        P(),
        P(),
        P(),
        P(),
        P(("nodes", "heads"), None, None),
        P(("nodes", "heads"), None),
        P(("nodes", "heads")),
    )
    return jax.shard_map(
        local, mesh=mesh, in_specs=placed, out_specs=P(("nodes", "heads"), None), check_vma=False
    )
```

time: 131 us -> 39.3 us (0.30)
  matrix products: 56 us -> 0 us
  local copies, waits for them, and re-layouts: 35.8 us -> 3.81 us
  other arithmetic: 11.4 us -> 0 us
  Pallas kernels: 0 us -> 10.1 us
  waiting for transfers between devices: 9.33 us -> 7.96 us
    dot_general x19 -> x0, matrix products: 44.2 us -> none  [the longest x8 19.8 us: local(): jnp.einsum('sqk,ske->sqe', weights, values, preferred_element_type=jnp.fl...]
    gather x10 -> x0, local copies, waits for them, and re-layouts: 21 us -> none  [the longest x8 20 us: local(): linked_parts.append(jnp.take(received, partner[:, link_index], axis=0))]
    sub x8 -> x0, matrix products: 11.8 us -> none  [local(): expo = jnp.exp(scores - top_score)]
    pallas_call x0 -> x3, Pallas kernels: none -> 10.1 us  [call(): pl.pallas_call(kernel, out_shape=outs, in_specs=[SMEM] * len(smem) + [VME...]
    reshape x4 -> x0, local copies, waits for them, and re-layouts: 8.56 us -> none  [local(): received = received.reshape(slot_count, block_rows, 2, width)]
    unnamed x3 -> x0, other arithmetic: 7.02 us -> none
    slice x3 -> x0, local copies, waits for them, and re-layouts: 2.11 us -> none  [the longest x1 0.96 us: local(): all_keys = jnp.concatenate([own_blocks[:, :, 1:]] + linked_parts, axis=1)]
    ppermute x4, waiting for transfers between devices: 9.33 us -> 7.96 us  [from_partner(): return lax.ppermute(value, axis, pairs)]
  transfers between devices with their start and end apart: 4 -> 4, of which waited for: 1 -> 1; matrix products, arithmetic and copies ran while one was open for 23% -> 0% of each run, Pallas kernels for 0% -> 15%
where the time goes in v1:
time: 39.3 us; the launch traced here: 38.9 us
  starting transfers between devices  16.3 us (41%)
  Pallas kernels  10.1 us (26%)
  waiting for transfers between devices  7.96 us (20%)
  local copies, waits for them, and re-layouts  3.81 us (10%)
  between operations  0.77 us (2%)
    ppermute x4, starting transfers between devices, from_partner(): return lax.ppermute(value, axis, pairs)  16.3 us
    pallas_call x3, Pallas kernels, call(): pl.pallas_call(kernel, out_shape=outs, in_specs=[SMEM] * len(smem) + [VME...  10.1 us
    ppermute x4, waiting for transfers between devices, from_partner(): return lax.ppermute(value, axis, pairs)  7.96 us
    unnamed x16, local copies, waits for them, and re-layouts  3.81 us
  transfers between devices with their start and end apart: 4, of which 1 were waited for; matrix products, arithmetic and copies ran while one was open for 0% of the time, Pallas kernels for 15%

profile of v1, /device:TPU:1, one launch (start us, length us, event | category | flops | bytes accessed | tf_op | source)
XLA Modules:
  0.0 38.9 jit_solution(12360650343646300556)
XLA Ops:
  0.0 8.8 %collective-permute-start.1 = (bf16[384,512]{1,0:T(8,128)(2,1)}, bf16[384,512]{1,0:T(8,128)(2,1)S(1)}, u32[]{:S(2)}, u32[]{:S(2)}) collective-permute-start(bf16[384,512]{1,0:T(8,128)(2,1)} %refs_8_.1), channel_id=1, source_target_pairs={{0,1},{1,0},{2,3},{3,2},{4,5},{5,4},{6,7},{7,6},{8,9},{9,8},{10,11... | collective-permute-start | bytes 1179656 | tf_op jit(solution)/shard_map/ppermute | solution.py:24
  8.8 1.9 %collective-permute-start.2 = (bf16[384,512]{1,0:T(8,128)(2,1)}, bf16[384,512]{1,0:T(8,128)(2,1)S(1)}, u32[]{:S(2)}, u32[]{:S(2)}) collective-permute-start(bf16[384,512]{1,0:T(8,128)(2,1)} %refs_8_.1), channel_id=1, source_target_pairs={{0,4},{2,6},{4,0},{6,2},{8,12},{10,14},{12,8},{14,10},{16,20},{18,... | collective-permute-start | bytes 1179656 | tf_op jit(solution)/shard_map/ppermute | solution.py:24
  10.7 1.9 %collective-permute-start.3 = (bf16[384,512]{1,0:T(8,128)(2,1)}, bf16[384,512]{1,0:T(8,128)(2,1)S(1)}, u32[]{:S(2)}, u32[]{:S(2)}) collective-permute-start(bf16[384,512]{1,0:T(8,128)(2,1)} %refs_8_.1), channel_id=1, source_target_pairs={{0,64},{2,66},{4,68},{6,70},{8,72},{10,74},{12,76},{14,78},{16,80}... | collective-permute-start | bytes 1179656 | tf_op jit(solution)/shard_map/ppermute | solution.py:24
  12.6 3.7 %collective-permute-start = (bf16[384,512]{1,0:T(8,128)(2,1)}, bf16[384,512]{1,0:T(8,128)(2,1)S(1)}, u32[]{:S(2)}, u32[]{:S(2)}) collective-permute-start(bf16[384,512]{1,0:T(8,128)(2,1)} %refs_8_.1), channel_id=1, source_target_pairs={{0,16},{2,18},{4,20},{6,22},{8,24},{10,26},{12,28},{14,30},{16,0},... | collective-permute-start | bytes 1179656 | tf_op jit(solution)/shard_map/ppermute | solution.py:24
  16.9 0.0 collective-permute-done.1.refs_2_
  17.0 0.0 copy-start
  17.0 1.4 %copy-done = bf16[512,3,512]{2,0,1:T(8,128)(2,1)S(1)} copy-done((bf16[512,3,512]{2,0,1:T(8,128)(2,1)S(1)}, bf16[512,3,512]{2,0,1:T(8,128)(2,1)}, u32[]{:S(2)}) %copy-start) | copy-done | bytes 1572888
  18.4 0.0 copy-start.5
  18.4 1.0 %copy-done.5 = bf16[384,512]{1,0:T(8,128)(2,1)S(1)} copy-done((bf16[384,512]{1,0:T(8,128)(2,1)S(1)}, bf16[384,512]{1,0:T(8,128)(2,1)}, u32[]{:S(2)}) %copy-start.5) | copy-done | bytes 393240
  19.4 0.0 copy-start.6
  19.4 0.7 %copy-done.6 = s32[3,4]{1,0:T(4,128)S(1)} copy-done((s32[3,4]{1,0:T(4,128)S(1)}, s32[3,4]{1,0:T(4,128)}, u32[]{:S(2)}) %copy-start.6) | copy-done | bytes 72
  20.0 0.0 copy-start.7
  20.0 0.7 %copy-done.7 = s32[3,128,8]{1,2,0:T(8,128)S(1)} copy-done((s32[3,128,8]{1,2,0:T(8,128)S(1)}, s32[3,128,8]{1,2,0:T(8,128)}, u32[]{:S(2)}) %copy-start.7) | copy-done | bytes 12312
  20.8 0.0 copy-start.1
  20.8 3.2 %own_and_core.1 = (bf16[384,512]{1,0:T(8,128)(2,1)S(1)}, f32[384,512]{1,0:T(8,128)S(1)}, f32[384,512]{1,0:T(8,128)S(1)}, f32[384,512]{1,0:T(8,128)S(1)}) custom-call(s32[3,4]{1,0:T(4,128)S(1)} %copy-done.6, bf16[384,512]{1,0:T(8,128)(2,1)S(1)} %copy-done.5, bf16[384,512]{1,0:T(8,128)(2,1)S(1)} %collective-permute-done.1.refs_2_, ...), custom_call_target="tpu_custom_call" | custom-call | flops 2000000000 | bytes 4194304 | tf_op jit(solution)/shard_map/own_and_core/pallas_call | solution.py:168
  24.0 0.0 collective-permute-done.2.refs_1_
  24.0 0.0 collective-permute-done.3.refs_2_
  24.0 0.0 copy-done.1
  24.0 0.0 copy-start.2
  24.0 0.0 copy-start.3
  24.1 0.0 copy-start.4
  24.1 2.8 %far_x_z.1 = (f32[384,512]{1,0:T(8,128)S(1)}, f32[384,512]{1,0:T(8,128)S(1)}, f32[384,512]{1,0:T(8,128)S(1)}) custom-call(s32[3,4]{1,0:T(4,128)S(1)} %copy-done.6, bf16[384,512]{1,0:T(8,128)(2,1)S(1)} %collective-permute-done.2.refs_1_, bf16[384,512]{1,0:T(8,128)(2,1)S(1)} %collective-permute-done.3.refs_2_, bf16[3,512,512]{2,1,0:T(8,128)(2,1)S(1)} %bitcast.3, ...), custom_call_target="tpu_custom_call" | custom-call | flops 2000000000 | bytes 4194304 | tf_op jit(solution)/shard_map/far_x_z/pallas_call | solution.py:168
  26.9 8.0 %collective-permute-done.refs_2_ = bf16[384,512]{1,0:T(8,128)(2,1)S(1)} collective-permute-done((bf16[384,512]{1,0:T(8,128)(2,1)}, bf16[384,512]{1,0:T(8,128)(2,1)S(1)}, u32[]{:S(2)}, u32[]{:S(2)}) %collective-permute-start) | collective-permute-done | bytes 393248 | tf_op jit(solution)/shard_map/ppermute | solution.py:24
  34.8 0.0 copy-done.2
  34.8 0.0 copy-done.3
  34.8 0.0 copy-done.4
  34.8 4.1 %far_y_mix.1 = bf16[384,512]{1,0:T(8,128)(2,1)} custom-call(s32[3,4]{1,0:T(4,128)S(1)} %copy-done.6, s32[1]{0:T(128)S(6)} %copy.9.refs_1_, bf16[384,512]{1,0:T(8,128)(2,1)S(1)} %collective-permute-done.refs_2_, bf16[3,512,512]{2,1,0:T(8,128)(2,1)S(1)} %bitcast.4, bf16[384,512]{1,0:T(8,128)(2,1)S(1)} %get-tuple-element.12.refs_4_, ...), custom_call_target="tpu_custom_call" | custom-call | flops 2000000000 | bytes 4194304 | tf_op jit(solution)/shard_map/far_y_mix/pallas_call | solution.py:168
Async XLA Ops:
  0.0 16.9 %collective-permute-start.1 = (bf16[384,512]{1,0:T(8,128)(2,1)}, bf16[384,512]{1,0:T(8,128)(2,1)S(1)}, u32[]{:S(2)}, u32[]{:S(2)}) collective-permute-start(bf16[384,512]{1,0:T(8,128)(2,1)} %refs_8_.1), channel_id=1, source_target_pairs={{0,1},{1,0},{2,3},{3,2},{4,5},{5,4},{6,7},{7,6},{8,9},{9,8},{10,11... | collective-permute-start | bytes 1179656 | tf_op jit(solution)/shard_map/ppermute | solution.py:24
  8.8 15.2 %collective-permute-start.2 = (bf16[384,512]{1,0:T(8,128)(2,1)}, bf16[384,512]{1,0:T(8,128)(2,1)S(1)}, u32[]{:S(2)}, u32[]{:S(2)}) collective-permute-start(bf16[384,512]{1,0:T(8,128)(2,1)} %refs_8_.1), channel_id=1, source_target_pairs={{0,4},{2,6},{4,0},{6,2},{8,12},{10,14},{12,8},{14,10},{16,20},{18,... | collective-permute-start | bytes 1179656 | tf_op jit(solution)/shard_map/ppermute | solution.py:24
  10.7 13.3 %collective-permute-start.3 = (bf16[384,512]{1,0:T(8,128)(2,1)}, bf16[384,512]{1,0:T(8,128)(2,1)S(1)}, u32[]{:S(2)}, u32[]{:S(2)}) collective-permute-start(bf16[384,512]{1,0:T(8,128)(2,1)} %refs_8_.1), channel_id=1, source_target_pairs={{0,64},{2,66},{4,68},{6,70},{8,72},{10,74},{12,76},{14,78},{16,80}... | collective-permute-start | bytes 1179656 | tf_op jit(solution)/shard_map/ppermute | solution.py:24
  12.6 22.2 %collective-permute-start = (bf16[384,512]{1,0:T(8,128)(2,1)}, bf16[384,512]{1,0:T(8,128)(2,1)S(1)}, u32[]{:S(2)}, u32[]{:S(2)}) collective-permute-start(bf16[384,512]{1,0:T(8,128)(2,1)} %refs_8_.1), channel_id=1, source_target_pairs={{0,16},{2,18},{4,20},{6,22},{8,24},{10,26},{12,28},{14,30},{16,0},... | collective-permute-start | bytes 1179656 | tf_op jit(solution)/shard_map/ppermute | solution.py:24
  17.0 1.4 %copy-start = (bf16[512,3,512]{2,0,1:T(8,128)(2,1)S(1)}, bf16[512,3,512]{2,0,1:T(8,128)(2,1)}, u32[]{:S(2)}) copy-start(bf16[512,3,512]{2,0,1:T(8,128)(2,1)} %param.9) | copy-start | bytes 4718596
  18.4 1.0 %copy-start.5 = (bf16[384,512]{1,0:T(8,128)(2,1)S(1)}, bf16[384,512]{1,0:T(8,128)(2,1)}, u32[]{:S(2)}) copy-start(bf16[384,512]{1,0:T(8,128)(2,1)} %refs_8_.1) | copy-start | bytes 1179652
  19.4 0.7 %copy-start.6 = (s32[3,4]{1,0:T(4,128)S(1)}, s32[3,4]{1,0:T(4,128)}, u32[]{:S(2)}) copy-start(s32[3,4]{1,0:T(4,128)} %refs_0_.5) | copy-start | bytes 148
  20.0 0.7 %copy-start.7 = (s32[3,128,8]{1,2,0:T(8,128)S(1)}, s32[3,128,8]{1,2,0:T(8,128)}, u32[]{:S(2)}) copy-start(s32[3,128,8]{1,2,0:T(8,128)} %param.13) | copy-start | bytes 36868
  20.8 3.3 %copy-start.1 = (bf16[512,3,512]{2,0,1:T(8,128)(2,1)S(1)}, bf16[512,3,512]{2,0,1:T(8,128)(2,1)}, u32[]{:S(2)}) copy-start(bf16[512,3,512]{2,0,1:T(8,128)(2,1)} %param.9) | copy-start | bytes 4718596
  24.0 10.8 %copy-start.2 = (bf16[512,1024]{1,0:T(8,128)(2,1)S(1)}, bf16[512,1024]{1,0:T(8,128)(2,1)}, u32[]{:S(2)}) copy-start(bf16[512,1024]{1,0:T(8,128)(2,1)} %refs_10_.1) | copy-start | bytes 3145732
  24.0 10.8 %copy-start.3 = (bf16[1024,512]{1,0:T(8,128)(2,1)S(1)}, bf16[1024,512]{1,0:T(8,128)(2,1)}, u32[]{:S(2)}) copy-start(bf16[1024,512]{1,0:T(8,128)(2,1)} %refs_11_.1) | copy-start | bytes 3145732
  24.1 10.8 %copy-start.4 = (bf16[512,512]{1,0:T(8,128)(2,1)S(1)}, bf16[512,512]{1,0:T(8,128)(2,1)}, u32[]{:S(2)}) copy-start(bf16[512,512]{1,0:T(8,128)(2,1)} %refs_9_.1) | copy-start | bytes 1572868

commit v2 on v0

v2 whole, which is shorter than its diff:
```python
import jax
import jax.numpy as jnp
from jax import lax
from jax.experimental import pallas as pl
from jax.experimental.pallas import tpu as pltpu
from jax.sharding import PartitionSpec as P

D = 512
H = 8
HEAD = D // H
BLK = 128
SLOTS = 3
ROWS = SLOTS * BLK
PAIRS = H // 2
EPSILON = 1e-05
SCALE = 1.4426950408889634 / HEAD**0.5
F32 = jnp.float32
BF16 = jnp.bfloat16


def from_partner(value, axis, bit):
    mask = 2**bit
    pairs = [(source, source ^ mask) for source in range(lax.axis_size(axis))]
    return lax.ppermute(value, axis, pairs)


def mm(a, b):
    return jnp.dot(a, b, preferred_element_type=F32)


def mm_nt(a, b):
    return lax.dot_general(a, b, (((1,), (1,)), ((), ())), preferred_element_type=F32)


def block(index):
    return slice(index * BLK, (index + 1) * BLK)


def head_rows(head):
    return slice(head * HEAD, (head + 1) * HEAD)


def local_mask(words):
    word_count = words.shape[0]
    halves = jnp.concatenate([words & 255, jnp.right_shift(words, 8)], axis=0).astype(F32).astype(BF16)
    key = lax.broadcasted_iota(jnp.int32, (BLK, 2 * word_count), 0)
    row = lax.broadcasted_iota(jnp.int32, (BLK, 2 * word_count), 1)
    source = key // 16 + word_count * (key % 16 // 8)
    pick = jnp.where(row == source, 1.0, 0.0).astype(BF16)
    picked = mm(pick, halves)
    key = lax.broadcasted_iota(jnp.int32, (BLK, BLK), 0)
    query = lax.broadcasted_iota(jnp.int32, (BLK, BLK), 1)
    bits = jnp.right_shift(picked.astype(jnp.int32), key % 8) & 1
    return (bits == 1) | (query == key)


def spread(q_pair):
    low = lax.broadcasted_iota(jnp.int32, q_pair.shape, 0) < HEAD
    zero = jnp.zeros_like(q_pair)
    return jnp.concatenate([jnp.where(low, q_pair, zero), jnp.where(low, zero, q_pair)], axis=1)


def attend(q_spread, keys, values, allowed):
    scores = jnp.concatenate([mm(keys(p), q_spread(p)) for p in range(PAIRS)], axis=1)
    if allowed is not None:
        scores = jnp.where(jnp.concatenate([allowed] * H, axis=1), scores, -1e30)
    top = jnp.max(scores, axis=0, keepdims=True)
    expo = jnp.exp2((scores - top) * SCALE)
    total = jnp.sum(expo, axis=0, keepdims=True)
    weights = expo.astype(BF16)
    return top, total, [mm(values[head_rows(h)], weights[:, block(h)]) for h in range(H)]


def project(x, wk, wvt, k_held, v_held):
    k_held[...] = mm(x, wk).astype(BF16)
    values = mm_nt(wvt, x).astype(BF16)
    for s in range(SLOTS):
        v_held[s] = values[:, block(s)]


def own_kernel(x_in, w, words, x_out, qs_out, wk_out, wvt_out, o_out, m_out, l_out, k_held, v_held):
    x = x_in.at[pl.ds(0, ROWS)]
    x_out[...] = x[...]
    wk_out[...] = w[1]
    wvt_out[...] = w[2].T
    project(x[...], wk_out[...], wvt_out[...], k_held, v_held)
    q = mm(x[...], w[0]).astype(BF16).T
    for s in range(SLOTS):
        for p in range(PAIRS):
            qs_out[s, p] = spread(q[block(p), block(s)])
        top, total, parts = attend(
            lambda p: qs_out[s, p], lambda p: k_held[block(s), block(p)], v_held[s], local_mask(words[s])
        )
        m_out[s] = top
        l_out[s] = total
        for h in range(H):
            o_out[head_rows(h), block(s)] = parts[h]


def merged(s, link, partner, qs, o_in, m_in, l_in, k_held, v_held):
    slot = partner[s, link]
    rows = pl.ds(pl.multiple_of(slot * BLK, BLK), BLK)
    top, total, parts = attend(lambda p: qs[s, p], lambda p: k_held[rows, block(p)], v_held[slot], None)
    m = jnp.maximum(m_in[s], top)
    old = jnp.exp2((m_in[s] - m) * SCALE)
    new = jnp.exp2((top - m) * SCALE)
    both = [
        o_in[head_rows(h), block(s)] * old[:, block(h)] + parts[h] * new[:, block(h)] for h in range(H)
    ]
    return m, l_in[s] * old + total * new, both


def far_kernel(link, partner_hbm, wk, wvt, qs, o_in, m_in, l_in, x, o_out, m_out, l_out, partner, k_held, v_held, sems):
    copy = pltpu.make_async_copy(partner_hbm, partner, sems.at[0])
    copy.start()
    if link == 0:
        other = pl.ds(pl.multiple_of((1 - lax.axis_index("heads")) * ROWS, ROWS), ROWS)
        x = x.at[other]
    project(x[...], wk[...], wvt[...], k_held, v_held)
    copy.wait()
    for s in range(SLOTS):
        m, l, both = merged(s, link, partner, qs, o_in, m_in, l_in, k_held, v_held)
        m_out[s] = m
        l_out[s] = l
        for h in range(H):
            o_out[head_rows(h), block(s)] = both[h]


def last_kernel(
    link, partner_hbm, counts_hbm, wk, wvt, qs, o_in, m_in, l_in, x, w_out, w_up, w_down, r, out,
    partner, counts, k_held, v_held, att, sems,
):
    copies = [
        pltpu.make_async_copy(partner_hbm, partner, sems.at[0]),
        pltpu.make_async_copy(counts_hbm, counts, sems.at[1]),
    ]
    for copy in copies:
        copy.start()
    project(r[pl.ds(0, ROWS)], wk[...], wvt[...], k_held, v_held)
    for copy in copies:
        copy.wait()
    for s in range(SLOTS):
        _, l, both = merged(s, link, partner, qs, o_in, m_in, l_in, k_held, v_held)
        share = 1.0 / l
        for p in range(PAIRS):
            pair = [both[h] * share[:, block(h)] for h in (2 * p, 2 * p + 1)]
            att[block(s), block(p)] = jnp.concatenate(pair, axis=0).astype(BF16).T
    resid = x[...].astype(F32) + mm(att[...], w_out[...])
    mean = jnp.mean(resid, axis=1, keepdims=True)
    var = jnp.mean(resid * resid, axis=1, keepdims=True) - mean * mean
    normed = (resid - mean) * lax.rsqrt(var + EPSILON)
    hidden = jnp.maximum(mm(normed.astype(BF16), w_up[...]), 0.0).astype(BF16)
    mixed = normed + mm(hidden, w_down[...])
    slot = lax.broadcasted_iota(jnp.int32, (ROWS, 1), 0) // BLK
    out[...] = jnp.where(slot < counts[0], mixed, 0.0).astype(BF16)


VMEM = pl.BlockSpec(memory_space=pltpu.VMEM)
ANY = pl.BlockSpec(memory_space=pltpu.HBM)
SPREAD = jax.ShapeDtypeStruct((SLOTS, PAIRS, BLK, 2 * BLK), BF16)
WEIGHT = jax.ShapeDtypeStruct((D, D), BF16)
STATE = (
    jax.ShapeDtypeStruct((D, ROWS), F32),
    jax.ShapeDtypeStruct((SLOTS, 1, H * BLK), F32),
    jax.ShapeDtypeStruct((SLOTS, 1, H * BLK), F32),
)
HELD = [pltpu.VMEM((ROWS, D), BF16), pltpu.VMEM((SLOTS, D, BLK), BF16)]
PARTNER = pltpu.SMEM((SLOTS, 4), jnp.int32)


PAD = 400


def stage_kernel(x, x_out):
    x_out[pl.ds(0, ROWS)] = x[...]


def stage(x):
    return pl.pallas_call(
        stage_kernel,
        out_shape=jax.ShapeDtypeStruct((PAD, D), BF16),
        in_specs=[VMEM],
        out_specs=VMEM,
        compiler_params=pltpu.CompilerParams(vmem_limit_bytes=4 * 2**20),
        cost_estimate=pl.CostEstimate(flops=0, bytes_accessed=8 * 2**20, transcendentals=0),
        name="stage",
    )(x)


def call(kernel, outside, inside, outs, scratch, name):
    return pl.pallas_call(
        kernel,
        out_shape=outs,
        in_specs=[ANY] * len(outside) + [VMEM] * len(inside),
        out_specs=jax.tree.map(lambda _: VMEM, outs),
        scratch_shapes=scratch,
        compiler_params=pltpu.CompilerParams(vmem_limit_bytes=12 * 2**20),
        cost_estimate=pl.CostEstimate(flops=0, bytes_accessed=0, transcendentals=0),
        name=name,
    )(*outside, *inside)


def local(features, w_qkv, w_out, w_up, w_down, pattern, partner, counts):
    log_size = (lax.axis_size("nodes") * lax.axis_size("heads")).bit_length() - 1
    bits = [link * log_size // 4 for link in range(4)]

    def exchange(value, link):
        bit = bits[link]
        return from_partner(value, "heads", 0) if bit == 0 else from_partner(value, "nodes", bit - 1)

    w = jnp.transpose(w_qkv, (1, 0, 2))
    words = jnp.transpose(pattern, (0, 2, 1))
    here = lax.axis_index("nodes") < lax.axis_size("nodes")

    def own(x):
        return call(
            own_kernel, [], [x, w, words], (jax.ShapeDtypeStruct((ROWS, D), BF16), SPREAD, WEIGHT, WEIGHT, *STATE),
            HELD, "own",
        )

    def far(link, x, fixed, state):
        return call(
            lambda *refs: far_kernel(link, *refs), [partner], [*fixed, *state, x], STATE,
            [PARTNER, *HELD, pltpu.SemaphoreType.DMA((1,))], "far",
        )

    def zeros(shapes):
        return tuple(jnp.zeros(shape.shape, shape.dtype) for shape in shapes)

    x = stage(features)
    received = {2: exchange(x, 2)}
    for link in (1, 3):
        received[link] = exchange(features, link)
    again, qs, wk, wvt, *state = own(x)
    fixed = (wk, wvt, qs)
    received[0] = lax.all_gather(again, "heads").reshape(2 * ROWS, D)
    for link in (0, 1, 3):
        state = far(link, received[link], fixed, state)
    parts = (*fixed, *state)
    received = received[2]
    return call(
        lambda *refs: last_kernel(2, *refs), [partner, counts], [*parts, again, w_out, w_up, w_down, received],
        jax.ShapeDtypeStruct((ROWS, D), BF16),
        [PARTNER, pltpu.SMEM((1,), jnp.int32), *HELD, pltpu.VMEM((ROWS, D), BF16), pltpu.SemaphoreType.DMA((2,))], "last",
    )


def solution(mesh):
    placed = (
        P(("nodes", "heads"), None),
        P(),
        P(),
        P(),
        P(),
        P(("nodes", "heads"), None, None),
        P(("nodes", "heads"), None),
        P(("nodes", "heads")),
    )
    return jax.shard_map(
        local, mesh=mesh, in_specs=placed, out_specs=P(("nodes", "heads"), None), check_vma=False
    )
```

time: 131 us -> 32.7 us (0.25)
  matrix products: 56 us -> 0 us
  local copies, waits for them, and re-layouts: 35.8 us -> 2.13 us
  Pallas kernels: 0 us -> 12.3 us
  other arithmetic: 11.4 us -> 0 us
  waiting for transfers between devices: 9.33 us -> 0.01 us
  blocking collectives: 0 us -> 3.51 us
  starting transfers between devices: 16.3 us -> 13.7 us
    dot_general x19 -> x0, matrix products: 44.2 us -> none  [the longest x8 19.8 us: local(): jnp.einsum('sqk,ske->sqe', weights, values, preferred_element_type=jnp.fl...]
    gather x10 -> x0, local copies, waits for them, and re-layouts: 21 us -> none  [the longest x8 20 us: local(): linked_parts.append(jnp.take(received, partner[:, link_index], axis=0))]
    pallas_call x0 -> x6, Pallas kernels: none -> 12.3 us  [the longest x5 11.2 us: call(): pl.pallas_call(kernel, out_shape=outs, in_specs=[ANY] * len(outside) + [V...]
    sub x8 -> x0, matrix products: 11.8 us -> none  [local(): expo = jnp.exp(scores - top_score)]
    ppermute x4 -> x3, waiting for transfers between devices: 9.33 us -> 0.01 us  [from_partner(): return lax.ppermute(value, axis, pairs)]
    reshape x4 -> x0, local copies, waits for them, and re-layouts: 8.56 us -> none  [local(): received = received.reshape(slot_count, block_rows, 2, width)]
    unnamed x3 -> x0, other arithmetic: 7.02 us -> none
    all_gather x0 -> x1, blocking collectives: none -> 3.51 us  [local(): received[0] = lax.all_gather(again, 'heads').reshape(2 * ROWS, D)]
  transfers between devices with their start and end apart: 4 -> 3, of which waited for: 1 -> 0; matrix products, arithmetic and copies ran while one was open for 23% -> 0% of each run, Pallas kernels for 0% -> 23%
where the time goes in v2:
time: 32.7 us; the launch traced here: 32.4 us
  starting transfers between devices  13.7 us (42%)
  Pallas kernels  12.3 us (38%)
  blocking collectives  3.51 us (11%)
  local copies, waits for them, and re-layouts  2.13 us (7%)
  between operations  0.79 us (2%)
    ppermute x3, starting transfers between devices, from_partner(): return lax.ppermute(value, axis, pairs)  13.7 us
    pallas_call x5, Pallas kernels, call(): pl.pallas_call(kernel, out_shape=outs, in_specs=[ANY] * len(outside) + [V...  11.2 us
    all_gather x1, blocking collectives, local(): received[0] = lax.all_gather(again, 'heads').reshape(2 * ROWS, D)  3.51 us
    unnamed x12, local copies, waits for them, and re-layouts  2.13 us
    pallas_call x1, Pallas kernels, stage(): pl.pallas_call(stage_kernel, out_shape=jax.ShapeDtypeStruct((PAD, D), BF1...  1.02 us
  transfers between devices with their start and end apart: 3, of which 0 were waited for; matrix products, arithmetic and copies ran while one was open for 0% of the time, Pallas kernels for 23%

profile of v2, /device:TPU:1, one launch (start us, length us, event | category | flops | bytes accessed | tf_op | source)
XLA Modules:
  0.0 32.4 jit_solution(4786284382954447281)
XLA Ops:
  0.0 1.0 %stage.1.x_in = bf16[400,512]{1,0:T(8,128)(2,1)S(1)} custom-call(bf16[384,512]{1,0:T(8,128)(2,1)} %x.1), custom_call_target="tpu_custom_call" | custom-call | bytes 8388608 | tf_op jit(solution)/shard_map/stage/pallas_call | solution.py:179
  1.0 5.0 %collective-permute-start.2 = (bf16[400,512]{1,0:T(8,128)(2,1)S(1)}, bf16[400,512]{1,0:T(8,128)(2,1)S(1)}, u32[]{:S(2)}, u32[]{:S(2)}) collective-permute-start(bf16[400,512]{1,0:T(8,128)(2,1)S(1)} %stage.1.x_in), channel_id=1, source_target_pairs={{0,16},{2,18},{4,20},{6,22},{8,24},{10,26},{12,28},{14,30},{16,0},... | collective-permute-start | bytes 1228808 | tf_op jit(solution)/shard_map/ppermute | solution.py:24
  6.1 4.7 %collective-permute-start = (bf16[384,512]{1,0:T(8,128)(2,1)}, bf16[384,512]{1,0:T(8,128)(2,1)S(1)}, u32[]{:S(2)}, u32[]{:S(2)}) collective-permute-start(bf16[384,512]{1,0:T(8,128)(2,1)} %x.1), channel_id=1, source_target_pairs={{0,4},{2,6},{4,0},{6,2},{8,12},{10,14},{12,8},{14,10},{16,20},{18,... | collective-permute-start | bytes 1179656 | tf_op jit(solution)/shard_map/ppermute | solution.py:24
  10.7 4.0 %collective-permute-start.1 = (bf16[384,512]{1,0:T(8,128)(2,1)}, bf16[384,512]{1,0:T(8,128)(2,1)S(1)}, u32[]{:S(2)}, u32[]{:S(2)}) collective-permute-start(bf16[384,512]{1,0:T(8,128)(2,1)} %x.1), channel_id=1, source_target_pairs={{0,64},{2,66},{4,68},{6,70},{8,72},{10,74},{12,76},{14,78},{16,80}... | collective-permute-start | bytes 1179656 | tf_op jit(solution)/shard_map/ppermute | solution.py:24
  15.4 0.0 copy-start
  15.4 1.4 %copy-done = bf16[512,3,512]{2,0,1:T(8,128)(2,1)S(1)} copy-done((bf16[512,3,512]{2,0,1:T(8,128)(2,1)S(1)}, bf16[512,3,512]{2,0,1:T(8,128)(2,1)}, u32[]{:S(2)}) %copy-start) | copy-done | bytes 1572888
  16.8 0.0 copy-start.5
  16.8 0.7 %copy-done.5 = s32[3,128,8]{1,2,0:T(8,128)S(1)} copy-done((s32[3,128,8]{1,2,0:T(8,128)S(1)}, s32[3,128,8]{1,2,0:T(8,128)}, u32[]{:S(2)}) %copy-start.5) | copy-done | bytes 12312
  17.5 0.0 copy-start.4
  17.5 2.0 %own.1 = (bf16[384,512]{1,0:T(8,128)(2,1)S(1)}, bf16[3,4,128,256]{3,2,1,0:T(8,128)(2,1)S(1)}, bf16[512,512]{1,0:T(8,128)(2,1)S(1)}, bf16[512,512]{1,0:T(8,128)(2...) custom-call(bf16[400,512]{1,0:T(8,128)(2,1)S(1)} %stage.1.x_in, ...), custom_call_target="tpu_custom_call" | custom-call | tf_op jit(solution)/shard_map/own/pallas_call | solution.py:191
  19.5 3.5 %all-gather.refs_7_ = bf16[768,512]{1,0:T(8,128)(2,1)S(1)} all-gather(bf16[384,512]{1,0:T(8,128)(2,1)S(1)} %get-tuple-element.27.refs_8_), channel_id=2, replica_groups=mesh['nodes'=256,'heads'=2] {'heads'}, dimensions={0}, use_global_device_ids=true | all-gather | bytes 1179648 | tf_op jit(solution)/shard_map/all_gather | solution.py:236
  23.0 0.0 copy-done.4
  23.0 1.8 %far.3 = (f32[512,384]{1,0:T(8,128)S(1)}, f32[3,1,1024]{2,1,0:T(1,128)S(1)}, f32[3,1,1024]{2,1,0:T(1,128)S(1)}) custom-call(s32[3,4]{1,0:T(4,128)S(1)} %copy-done.4, bf16[512,512]{1,0:T(8,128)(2,1)S(1)} %get-tuple-element.21.refs_1_.refs_2_, bf16[512,512]{1,0:T(8,128)(2,1)S(1)} %get-tuple-element.22.refs_2_.refs_3_, ...), custom_call_target="tpu_custom_call" | custom-call | tf_op jit(solution)/shard_map/far/pallas_call | solution.py:191
  24.8 0.0 collective-permute-done.refs_7_
  24.8 1.8 %far.4 = (f32[512,384]{1,0:T(8,128)S(1)}, f32[3,1,1024]{2,1,0:T(1,128)S(1)}, f32[3,1,1024]{2,1,0:T(1,128)S(1)}) custom-call(s32[3,4]{1,0:T(4,128)S(1)} %copy-done.4, bf16[512,512]{1,0:T(8,128)(2,1)S(1)} %get-tuple-element.21.refs_1_.refs_2_, bf16[512,512]{1,0:T(8,128)(2,1)S(1)} %get-tuple-element.22.refs_2_.refs_3_, ...), custom_call_target="tpu_custom_call" | custom-call | tf_op jit(solution)/shard_map/far/pallas_call | solution.py:191
  26.6 0.0 copy-start.1
  26.6 0.0 copy-start.2
  26.6 0.0 copy-start.3
  26.7 0.0 collective-permute-done.1.refs_7_
  26.7 1.8 %far.5 = (f32[512,384]{1,0:T(8,128)S(1)}, f32[3,1,1024]{2,1,0:T(1,128)S(1)}, f32[3,1,1024]{2,1,0:T(1,128)S(1)}) custom-call(s32[3,4]{1,0:T(4,128)S(1)} %copy-done.4, bf16[512,512]{1,0:T(8,128)(2,1)S(1)} %get-tuple-element.21.refs_1_.refs_2_, bf16[512,512]{1,0:T(8,128)(2,1)S(1)} %get-tuple-element.22.refs_2_.refs_3_, ...), custom_call_target="tpu_custom_call" | custom-call | tf_op jit(solution)/shard_map/far/pallas_call | solution.py:191
  28.5 0.0 collective-permute-done.2.refs_12_
  28.5 0.0 copy-done.1
  28.5 0.0 copy-done.2
  28.5 0.0 copy-done.3
  28.5 3.9 %last.1 = bf16[384,512]{1,0:T(8,128)(2,1)} custom-call(s32[3,4]{1,0:T(4,128)S(1)} %copy-done.4, s32[1]{0:T(128)S(6)} %copy.9.refs_1_, bf16[512,512]{1,0:T(8,128)(2,1)S(1)} %get-tuple-element.21.refs_1_.refs_2_, bf16[512,512]{1,0:T(8,128)(2,1)S(1)} %get-tuple-element.22.refs_2_.refs_3_, bf16[3,4,128,256]{3,2,1,0:T(8,128)(2,1)S(1)} %get-tuple-element.23.refs_3_.refs_4_, ...), custom_call_target="tpu_custom_call" | custom-call | tf_op jit(solution)/shard_map/last/pallas_call | solution.py:191
Async XLA Ops:
  1.0 27.5 %collective-permute-start.2 = (bf16[400,512]{1,0:T(8,128)(2,1)S(1)}, bf16[400,512]{1,0:T(8,128)(2,1)S(1)}, u32[]{:S(2)}, u32[]{:S(2)}) collective-permute-start(bf16[400,512]{1,0:T(8,128)(2,1)S(1)} %stage.1.x_in), channel_id=1, source_target_pairs={{0,16},{2,18},{4,20},{6,22},{8,24},{10,26},{12,28},{14,30},{16,0},... | collective-permute-start | bytes 1228808 | tf_op jit(solution)/shard_map/ppermute | solution.py:24
  6.1 18.7 %collective-permute-start = (bf16[384,512]{1,0:T(8,128)(2,1)}, bf16[384,512]{1,0:T(8,128)(2,1)S(1)}, u32[]{:S(2)}, u32[]{:S(2)}) collective-permute-start(bf16[384,512]{1,0:T(8,128)(2,1)} %x.1), channel_id=1, source_target_pairs={{0,4},{2,6},{4,0},{6,2},{8,12},{10,14},{12,8},{14,10},{16,20},{18,... | collective-permute-start | bytes 1179656 | tf_op jit(solution)/shard_map/ppermute | solution.py:24
  10.7 15.9 %collective-permute-start.1 = (bf16[384,512]{1,0:T(8,128)(2,1)}, bf16[384,512]{1,0:T(8,128)(2,1)S(1)}, u32[]{:S(2)}, u32[]{:S(2)}) collective-permute-start(bf16[384,512]{1,0:T(8,128)(2,1)} %x.1), channel_id=1, source_target_pairs={{0,64},{2,66},{4,68},{6,70},{8,72},{10,74},{12,76},{14,78},{16,80}... | collective-permute-start | bytes 1179656 | tf_op jit(solution)/shard_map/ppermute | solution.py:24
  15.4 1.4 %copy-start = (bf16[512,3,512]{2,0,1:T(8,128)(2,1)S(1)}, bf16[512,3,512]{2,0,1:T(8,128)(2,1)}, u32[]{:S(2)}) copy-start(bf16[512,3,512]{2,0,1:T(8,128)(2,1)} %param.9) | copy-start | bytes 4718596
  16.8 0.7 %copy-start.5 = (s32[3,128,8]{1,2,0:T(8,128)S(1)}, s32[3,128,8]{1,2,0:T(8,128)}, u32[]{:S(2)}) copy-start(s32[3,128,8]{1,2,0:T(8,128)} %param.13) | copy-start | bytes 36868
  17.5 5.5 %copy-start.4 = (s32[3,4]{1,0:T(4,128)S(1)}, s32[3,4]{1,0:T(4,128)}, u32[]{:S(2)}) copy-start(s32[3,4]{1,0:T(4,128)} %refs_0_.7) | copy-start | bytes 148
  26.6 1.9 %copy-start.1 = (bf16[512,1024]{1,0:T(8,128)(2,1)S(1)}, bf16[512,1024]{1,0:T(8,128)(2,1)}, u32[]{:S(2)}) copy-start(bf16[512,1024]{1,0:T(8,128)(2,1)} %refs_10_.1) | copy-start | bytes 3145732
  26.6 1.9 %copy-start.2 = (bf16[1024,512]{1,0:T(8,128)(2,1)S(1)}, bf16[1024,512]{1,0:T(8,128)(2,1)}, u32[]{:S(2)}) copy-start(bf16[1024,512]{1,0:T(8,128)(2,1)} %refs_11_.1) | copy-start | bytes 3145732
  26.6 1.9 %copy-start.3 = (bf16[512,512]{1,0:T(8,128)(2,1)S(1)}, bf16[512,512]{1,0:T(8,128)(2,1)}, u32[]{:S(2)}) copy-start(bf16[512,512]{1,0:T(8,128)(2,1)} %refs_9_.1) | copy-start | bytes 1572868

commit v3 on v2

v3 whole, which is shorter than its diff:
```python
import jax
import jax.numpy as jnp
from jax import lax
from jax.experimental import pallas as pl
from jax.experimental.pallas import tpu as pltpu
from jax.sharding import PartitionSpec as P

D = 512
H = 8
HEAD = D // H
BLK = 128
SLOTS = 3
ROWS = SLOTS * BLK
PAIRS = H // 2
EPSILON = 1e-05
SCALE = 1.4426950408889634 / HEAD**0.5
F32 = jnp.float32
BF16 = jnp.bfloat16


def from_partner(value, axis, bit):
    mask = 2**bit
    pairs = [(source, source ^ mask) for source in range(lax.axis_size(axis))]
    return lax.ppermute(value, axis, pairs)


def mm(a, b):
    return jnp.dot(a, b, preferred_element_type=F32)


def mm_nt(a, b):
    return lax.dot_general(a, b, (((1,), (1,)), ((), ())), preferred_element_type=F32)


def block(index):
    return slice(index * BLK, (index + 1) * BLK)


def head_rows(head):
    return slice(head * HEAD, (head + 1) * HEAD)


def local_mask(words):
    word_count = words.shape[0]
    halves = jnp.concatenate([words & 255, jnp.right_shift(words, 8)], axis=0).astype(F32).astype(BF16)
    key = lax.broadcasted_iota(jnp.int32, (BLK, 2 * word_count), 0)
    row = lax.broadcasted_iota(jnp.int32, (BLK, 2 * word_count), 1)
    source = key // 16 + word_count * (key % 16 // 8)
    pick = jnp.where(row == source, 1.0, 0.0).astype(BF16)
    picked = mm(pick, halves)
    key = lax.broadcasted_iota(jnp.int32, (BLK, BLK), 0)
    query = lax.broadcasted_iota(jnp.int32, (BLK, BLK), 1)
    bits = jnp.right_shift(picked.astype(jnp.int32), key % 8) & 1
    return (bits == 1) | (query == key)


def spread(q_pair):
    low = lax.broadcasted_iota(jnp.int32, q_pair.shape, 0) < HEAD
    zero = jnp.zeros_like(q_pair)
    return jnp.concatenate([jnp.where(low, q_pair, zero), jnp.where(low, zero, q_pair)], axis=1)


def attend(q_spread, sources):
    scores = []
    for keys, _, allowed in sources:
        score = jnp.concatenate([mm(keys(p), q_spread(p)) for p in range(PAIRS)], axis=1)
        if allowed is not None:
            score = jnp.where(jnp.concatenate([allowed] * H, axis=1), score, -1e30)
        scores.append(score)
    scores = jnp.concatenate(scores, axis=0)
    values = jnp.concatenate([values for _, values, _ in sources], axis=1)
    top = jnp.max(scores, axis=0, keepdims=True)
    expo = jnp.exp2((scores - top) * SCALE)
    total = jnp.sum(expo, axis=0, keepdims=True)
    weights = expo.astype(BF16)
    return top, total, [mm(values[head_rows(h)], weights[:, block(h)]) for h in range(H)]


def project(x, wk, wvt, k_held, v_held):
    k_held[...] = mm(x, wk).astype(BF16)
    values = mm_nt(wvt, x).astype(BF16)
    for s in range(x.shape[0] // BLK):
        v_held[s] = values[:, block(s)]


def named_slot(partner, s, link):
    row = lax.broadcasted_iota(jnp.int32, partner.shape, 0)
    column = lax.broadcasted_iota(jnp.int32, partner.shape, 1)
    return jnp.max(jnp.where((row == s) & (column == link), partner[...].astype(F32), 0.0)).astype(jnp.int32)


def far_source(slot, k_held, v_held):
    rows = pl.ds(pl.multiple_of(slot * BLK, BLK), BLK)
    return lambda p: k_held[rows, block(p)], v_held[slot], None


def own_kernel(partner, both, w, words, qs_out, wk_out, wvt_out, o_out, m_out, l_out, k_held, v_held):
    core = lax.axis_index("heads")
    wk_out[...] = w[1]
    wvt_out[...] = w[2].T
    project(both[...], wk_out[...], wvt_out[...], k_held, v_held)
    q = mm(both[pl.ds(pl.multiple_of(core * ROWS, ROWS), ROWS)], w[0]).astype(BF16).T
    for s in range(SLOTS):
        for p in range(PAIRS):
            qs_out[s, p] = spread(q[block(p), block(s)])
        own_keys, own_values, _ = far_source(core * SLOTS + s, k_held, v_held)
        beside = far_source((1 - core) * SLOTS + named_slot(partner, s, 0), k_held, v_held)
        top, total, parts = attend(lambda p: qs_out[s, p], [(own_keys, own_values, local_mask(words[s])), beside])
        m_out[s] = top
        l_out[s] = total
        for h in range(H):
            o_out[head_rows(h), block(s)] = parts[h]


def pair_block(pair):
    return slice(2 * pair * BLK, 2 * (pair + 1) * BLK)


def merged(s, p, keys, values, qs, o_in, m_in, l_in):
    scores = mm(keys(p), qs[s, p])
    top = jnp.max(scores, axis=0, keepdims=True)
    m_old = m_in[s, :, pair_block(p)]
    m = jnp.maximum(m_old, top)
    old = jnp.exp2((m_old - m) * SCALE)
    expo = jnp.exp2((scores - m) * SCALE)
    l = l_in[s, :, pair_block(p)] * old + jnp.sum(expo, axis=0, keepdims=True)
    weights = expo.astype(BF16)
    o = [
        o_in[head_rows(2 * p + i), block(s)] * old[:, block(i)] + mm(values[head_rows(2 * p + i)], weights[:, block(i)])
        for i in range(2)
    ]
    return m, l, o


def far_kernel(link, partner, wk, wvt, qs, o_in, m_in, l_in, x, o_out, m_out, l_out, k_held, v_held):
    project(x[...], wk[...], wvt[...], k_held, v_held)
    for s in range(SLOTS):
        keys, values, _ = far_source(named_slot(partner, s, link), k_held, v_held)
        for p in range(PAIRS):
            m, l, o = merged(s, p, keys, values, qs, o_in, m_in, l_in)
            m_out[s, :, pair_block(p)] = m
            l_out[s, :, pair_block(p)] = l
            for i in range(2):
                o_out[head_rows(2 * p + i), block(s)] = o[i]


def last_kernel(
    link, partner, counts, wk, wvt, qs, o_in, m_in, l_in, both_x, w_out, w_up, w_down, r, out, k_held, v_held, att, done, sems,
):
    core = lax.axis_index("heads")
    project(r[pl.ds(0, ROWS)], wk[...], wvt[...], k_held, v_held)
    for s in range(SLOTS):
        keys, values, _ = far_source(named_slot(partner, s, link), k_held, v_held)
        for p in range(PAIRS):
            _, l, o = merged(s, p, keys, values, qs, o_in, m_in, l_in)
            share = 1.0 / l
            o = jnp.concatenate([o[i] * share[:, block(i)] for i in range(2)], axis=0)
            att[block(s), block(p)] = o.astype(BF16).T
    x = both_x[pl.ds(pl.multiple_of(core * ROWS, ROWS), ROWS)]
    resid = x.astype(F32) + mm(att[...], w_out[...])
    mean = jnp.mean(resid, axis=1, keepdims=True)
    var = jnp.mean(resid * resid, axis=1, keepdims=True) - mean * mean
    normed = (resid - mean) * lax.rsqrt(var + EPSILON)
    hidden = jnp.maximum(mm(normed.astype(BF16), w_up[...]), 0.0).astype(BF16)
    copies = []
    for s in range(SLOTS):
        mixed = normed[block(s)] + mm(hidden[block(s)], w_down[...])
        done[block(s)] = jnp.where(s < counts[...], mixed, 0.0).astype(BF16)
        copies.append(pltpu.make_async_copy(done.at[block(s)], out.at[block(s)], sems.at[s]))
        copies[s].start()
    for copy in copies:
        copy.wait()


VMEM = pl.BlockSpec(memory_space=pltpu.VMEM)
SMEM = pl.BlockSpec(memory_space=pltpu.SMEM)
SPREAD = jax.ShapeDtypeStruct((SLOTS, PAIRS, BLK, 2 * BLK), BF16)
WEIGHT = jax.ShapeDtypeStruct((D, D), BF16)
STATE = (
    jax.ShapeDtypeStruct((D, ROWS), F32),
    jax.ShapeDtypeStruct((SLOTS, 1, H * BLK), F32),
    jax.ShapeDtypeStruct((SLOTS, 1, H * BLK), F32),
)
HELD = [pltpu.VMEM((ROWS, D), BF16), pltpu.VMEM((SLOTS, D, BLK), BF16)]
BOTH_HELD = [pltpu.VMEM((2 * ROWS, D), BF16), pltpu.VMEM((2 * SLOTS, D, BLK), BF16)]


PAD = 400


def stage_kernel(x, x_out, sems):
    copies = [
        pltpu.make_async_copy(x, x_out.at[pl.ds(0, ROWS)], sems.at[0]),
        pltpu.make_async_copy(x.at[pl.ds(0, PAD - ROWS)], x_out.at[pl.ds(ROWS, PAD - ROWS)], sems.at[1]),
    ]
    for copy in copies:
        copy.start()
    for copy in copies:
        copy.wait()


def stage(x):
    return pl.pallas_call(
        stage_kernel,
        out_shape=jax.ShapeDtypeStruct((PAD, D), BF16),
        in_specs=[pl.BlockSpec(memory_space=pltpu.HBM)],
        out_specs=VMEM,
        scratch_shapes=[pltpu.SemaphoreType.DMA((2,))],
        compiler_params=pltpu.CompilerParams(vmem_limit_bytes=4 * 2**20),
        cost_estimate=pl.CostEstimate(flops=0, bytes_accessed=8 * 2**20, transcendentals=0),
        name="stage",
    )(x)


def call(kernel, scalars, inside, outs, scratch, name, out_space=pltpu.VMEM):
    return pl.pallas_call(
        kernel,
        out_shape=outs,
        in_specs=[VMEM] * (len(scalars) + len(inside)),
        out_specs=jax.tree.map(lambda _: pl.BlockSpec(memory_space=out_space), outs),
        scratch_shapes=scratch,
        compiler_params=pltpu.CompilerParams(vmem_limit_bytes=12 * 2**20),
        cost_estimate=pl.CostEstimate(flops=0, bytes_accessed=0, transcendentals=0),
        name=name,
    )(*scalars, *inside)


def local(features, w_qkv, w_out, w_up, w_down, pattern, partner, counts):
    log_size = (lax.axis_size("nodes") * lax.axis_size("heads")).bit_length() - 1
    bits = [link * log_size // 4 for link in range(4)]

    def exchange(value, link):
        return from_partner(value, "nodes", bits[link] - 1)

    w = jnp.transpose(w_qkv, (1, 0, 2))
    words = jnp.transpose(pattern, (0, 2, 1))
    received = {2: exchange(stage(features), 2)}
    for link in (1, 3):
        received[link] = exchange(features, link)
    both = lax.all_gather(features, "heads").reshape(2 * ROWS, D)
    qs, wk, wvt, *state = call(
        own_kernel, [partner], [both, w, words], (SPREAD, WEIGHT, WEIGHT, *STATE), BOTH_HELD, "own"
    )
    fixed = (wk, wvt, qs)
    for link in (1, 3):
        state = call(
            lambda *refs, link=link: far_kernel(link, *refs), [partner], [*fixed, *state, received[link]], STATE, HELD, "far"
        )
    return call(
        lambda *refs: last_kernel(2, *refs), [partner, counts.reshape(1, 1)],
        [*fixed, *state, both, w_out, w_up, w_down, received[2]],
        jax.ShapeDtypeStruct((ROWS, D), BF16),
        [*HELD, *[pltpu.VMEM((ROWS, D), BF16)] * 2, pltpu.SemaphoreType.DMA((SLOTS,))], "last", pltpu.HBM,
    )


def solution(mesh):
    placed = (
        P(("nodes", "heads"), None),
        P(),
        P(),
        P(),
        P(),
        P(("nodes", "heads"), None, None),
        P(("nodes", "heads"), None),
        P(("nodes", "heads")),
    )
    return jax.shard_map(
        local, mesh=mesh, in_specs=placed, out_specs=P(("nodes", "heads"), None), check_vma=False
    )
```

time: 32.7 us -> 28.5 us (0.87)
  Pallas kernels: 12.3 us -> 9.67 us
  local copies, waits for them, and re-layouts: 2.13 us -> 0.37 us
    pallas_call x5 -> x4, Pallas kernels: 11.2 us -> 8.54 us  [call(): pl.pallas_call(kernel, out_shape=outs, in_specs=[VMEM] * (len(scalars) +...]
    unnamed x12, local copies, waits for them, and re-layouts: 2.13 us -> 0.37 us
  transfers between devices with their start and end apart: 3 -> 3, of which waited for: 0 -> 0; matrix products, arithmetic and copies ran while one was open for 0% -> 0% of each run, Pallas kernels for 23% -> 19%
where the time goes in v3:
time: 28.5 us; the launch traced here: 28.2 us
  starting transfers between devices  13.7 us (48%)
  Pallas kernels  9.67 us (34%)
  blocking collectives  3.72 us (13%)
  between operations  0.75 us (3%)
  local copies, waits for them, and re-layouts  0.37 us (1%)
    ppermute x3, starting transfers between devices, from_partner(): return lax.ppermute(value, axis, pairs)  13.7 us
    pallas_call x4, Pallas kernels, call(): pl.pallas_call(kernel, out_shape=outs, in_specs=[VMEM] * (len(scalars) +...  8.54 us
    all_gather x1, blocking collectives, local(): both = lax.all_gather(features, 'heads').reshape(2 * ROWS, D)  3.72 us
    pallas_call x1, Pallas kernels, stage(): pl.pallas_call(stage_kernel, out_shape=jax.ShapeDtypeStruct((PAD, D), BF1...  1.13 us
  transfers between devices with their start and end apart: 3, of which 0 were waited for; matrix products, arithmetic and copies ran while one was open for 0% of the time, Pallas kernels for 19%

profile of v3, /device:TPU:1, one launch (start us, length us, event | category | flops | bytes accessed | tf_op | source)
XLA Modules:
  0.0 28.2 jit_solution(13997754551801363066)
XLA Ops:
  0.0 0.0 copy-start
  0.0 0.0 copy-start.5
  0.0 0.0 copy-start.4
  0.0 1.1 %stage.1 = bf16[400,512]{1,0:T(8,128)(2,1)S(1)} custom-call(bf16[384,512]{1,0:T(8,128)(2,1)} %x.1), custom_call_target="tpu_custom_call" | custom-call | bytes 8388608 | tf_op jit(solution)/shard_map/stage/pallas_call | solution.py:203
  1.2 5.0 %collective-permute-start.2 = (bf16[400,512]{1,0:T(8,128)(2,1)S(1)}, bf16[400,512]{1,0:T(8,128)(2,1)S(1)}, u32[]{:S(2)}, u32[]{:S(2)}) collective-permute-start(bf16[400,512]{1,0:T(8,128)(2,1)S(1)} %stage.1), channel_id=1, source_target_pairs={{0,16},{2,18},{4,20},{6,22},{8,24},{10,26},{12,28},{14,30},{16,0},... | collective-permute-start | bytes 1228808 | tf_op jit(solution)/shard_map/ppermute | solution.py:24
  6.2 4.7 %collective-permute-start = (bf16[384,512]{1,0:T(8,128)(2,1)}, bf16[384,512]{1,0:T(8,128)(2,1)S(1)}, u32[]{:S(2)}, u32[]{:S(2)}) collective-permute-start(bf16[384,512]{1,0:T(8,128)(2,1)} %x.1), channel_id=1, source_target_pairs={{0,4},{2,6},{4,0},{6,2},{8,12},{10,14},{12,8},{14,10},{16,20},{18,... | collective-permute-start | bytes 1179656 | tf_op jit(solution)/shard_map/ppermute | solution.py:24
  10.9 4.0 %collective-permute-start.1 = (bf16[384,512]{1,0:T(8,128)(2,1)}, bf16[384,512]{1,0:T(8,128)(2,1)S(1)}, u32[]{:S(2)}, u32[]{:S(2)}) collective-permute-start(bf16[384,512]{1,0:T(8,128)(2,1)} %x.1), channel_id=1, source_target_pairs={{0,64},{2,66},{4,68},{6,70},{8,72},{10,74},{12,76},{14,78},{16,80}... | collective-permute-start | bytes 1179656 | tf_op jit(solution)/shard_map/ppermute | solution.py:24
  15.5 3.7 %all-gather.both.refs_8_ = bf16[768,512]{1,0:T(8,128)(2,1)S(1)} all-gather(bf16[384,512]{1,0:T(8,128)(2,1)} %x.1), channel_id=2, replica_groups=mesh['nodes'=256,'heads'=2] {'heads'}, dimensions={0}, use_global_device_ids=true | all-gather | bytes 1179648 | tf_op jit(solution)/shard_map/all_gather | solution.py:240
  19.2 0.0 copy-done
  19.3 0.0 copy-done.5
  19.3 0.0 copy-done.4
  19.3 2.7 %own.1 = (bf16[3,4,128,256]{3,2,1,0:T(8,128)(2,1)S(1)}, bf16[512,512]{1,0:T(8,128)(2,1)S(1)}, bf16[512,512]{1,0:T(8,128)(2,1)S(1)}, f32[512,384]{1,0:T(8,128)S(1...) custom-call(s32[3,4]{1,0:T(4,128)S(1)} %copy-done.4, bf16[768,512]{1,0:T(8,128)(2,1)S(1)} %all-gather.both.refs_8_, ...), custom_call_target="tpu_custom_call" | custom-call | tf_op jit(solution)/shard_map/own/pallas_call | solution.py:216
  22.0 0.0 collective-permute-done.refs_7_
  22.0 1.3 %far.2 = (f32[512,384]{1,0:T(8,128)S(1)}, f32[3,1,1024]{2,1,0:T(1,128)S(1)}, f32[3,1,1024]{2,1,0:T(1,128)S(1)}) custom-call(s32[3,4]{1,0:T(4,128)S(1)} %copy-done.4, bf16[512,512]{1,0:T(8,128)(2,1)S(1)} %get-tuple-element.17.refs_1_.refs_2_, bf16[512,512]{1,0:T(8,128)(2,1)S(1)} %get-tuple-element.18.refs_2_.refs_3_, ...), custom_call_target="tpu_custom_call" | custom-call | tf_op jit(solution)/shard_map/far/pallas_call | solution.py:216
  23.3 0.0 copy-start.1
  23.3 0.0 copy-start.2
  23.3 0.0 copy-start.3
  23.3 0.0 collective-permute-done.1.refs_7_
  23.3 1.3 %far.3 = (f32[512,384]{1,0:T(8,128)S(1)}, f32[3,1,1024]{2,1,0:T(1,128)S(1)}, f32[3,1,1024]{2,1,0:T(1,128)S(1)}) custom-call(s32[3,4]{1,0:T(4,128)S(1)} %copy-done.4, bf16[512,512]{1,0:T(8,128)(2,1)S(1)} %get-tuple-element.17.refs_1_.refs_2_, bf16[512,512]{1,0:T(8,128)(2,1)S(1)} %get-tuple-element.18.refs_2_.refs_3_, ...), custom_call_target="tpu_custom_call" | custom-call | tf_op jit(solution)/shard_map/far/pallas_call | solution.py:216
  24.6 0.0 collective-permute-done.2.refs_12_
  24.6 0.0 copy-done.1
  24.6 0.2 copy-done.2
  24.8 0.1 copy-done.3
  25.0 3.3 %last.1 = bf16[384,512]{1,0:T(8,128)(2,1)} custom-call(s32[3,4]{1,0:T(4,128)S(1)} %copy-done.4, s32[1,1]{1,0:T(1,128)} %bitcast.3.refs_1_, bf16[512,512]{1,0:T(8,128)(2,1)S(1)} %get-tuple-element.17.refs_1_.refs_2_, bf16[512,512]{1,0:T(8,128)(2,1)S(1)} %get-tuple-element.18.refs_2_.refs_3_, bf16[3,4,128,256]{3,2,1,0:T(8,128)(2,1)S(1)} %get-tuple-element.19.refs_3_.refs_4_, ...), custom_call_target="tpu_custom_call" | custom-call | tf_op jit(solution)/shard_map/last/pallas_call | solution.py:216
Async XLA Ops:
  0.0 19.3 %copy-start = (bf16[512,3,512]{2,0,1:T(8,128)(2,1)S(1)}, bf16[512,3,512]{2,0,1:T(8,128)(2,1)}, u32[]{:S(2)}) copy-start(bf16[512,3,512]{2,0,1:T(8,128)(2,1)} %param.9) | copy-start | bytes 4718596
  0.0 19.3 %copy-start.5 = (s32[3,128,8]{1,2,0:T(8,128)S(1)}, s32[3,128,8]{1,2,0:T(8,128)}, u32[]{:S(2)}) copy-start(s32[3,128,8]{1,2,0:T(8,128)} %param.13) | copy-start | bytes 36868
  0.0 19.3 %copy-start.4 = (s32[3,4]{1,0:T(4,128)S(1)}, s32[3,4]{1,0:T(4,128)}, u32[]{:S(2)}) copy-start(s32[3,4]{1,0:T(4,128)} %refs_0_.5) | copy-start | bytes 148
  1.2 23.4 %collective-permute-start.2 = (bf16[400,512]{1,0:T(8,128)(2,1)S(1)}, bf16[400,512]{1,0:T(8,128)(2,1)S(1)}, u32[]{:S(2)}, u32[]{:S(2)}) collective-permute-start(bf16[400,512]{1,0:T(8,128)(2,1)S(1)} %stage.1), channel_id=1, source_target_pairs={{0,16},{2,18},{4,20},{6,22},{8,24},{10,26},{12,28},{14,30},{16,0},... | collective-permute-start | bytes 1228808 | tf_op jit(solution)/shard_map/ppermute | solution.py:24
  6.2 15.8 %collective-permute-start = (bf16[384,512]{1,0:T(8,128)(2,1)}, bf16[384,512]{1,0:T(8,128)(2,1)S(1)}, u32[]{:S(2)}, u32[]{:S(2)}) collective-permute-start(bf16[384,512]{1,0:T(8,128)(2,1)} %x.1), channel_id=1, source_target_pairs={{0,4},{2,6},{4,0},{6,2},{8,12},{10,14},{12,8},{14,10},{16,20},{18,... | collective-permute-start | bytes 1179656 | tf_op jit(solution)/shard_map/ppermute | solution.py:24
  10.9 12.5 %collective-permute-start.1 = (bf16[384,512]{1,0:T(8,128)(2,1)}, bf16[384,512]{1,0:T(8,128)(2,1)S(1)}, u32[]{:S(2)}, u32[]{:S(2)}) collective-permute-start(bf16[384,512]{1,0:T(8,128)(2,1)} %x.1), channel_id=1, source_target_pairs={{0,64},{2,66},{4,68},{6,70},{8,72},{10,74},{12,76},{14,78},{16,80}... | collective-permute-start | bytes 1179656 | tf_op jit(solution)/shard_map/ppermute | solution.py:24
  23.3 1.3 %copy-start.1 = (bf16[512,1024]{1,0:T(8,128)(2,1)S(1)}, bf16[512,1024]{1,0:T(8,128)(2,1)}, u32[]{:S(2)}) copy-start(bf16[512,1024]{1,0:T(8,128)(2,1)} %refs_10_.1) | copy-start | bytes 3145732
  23.3 1.5 %copy-start.2 = (bf16[1024,512]{1,0:T(8,128)(2,1)S(1)}, bf16[1024,512]{1,0:T(8,128)(2,1)}, u32[]{:S(2)}) copy-start(bf16[1024,512]{1,0:T(8,128)(2,1)} %refs_11_.1) | copy-start | bytes 3145732
  23.3 1.7 %copy-start.3 = (bf16[512,512]{1,0:T(8,128)(2,1)S(1)}, bf16[512,512]{1,0:T(8,128)(2,1)}, u32[]{:S(2)}) copy-start(bf16[512,512]{1,0:T(8,128)(2,1)} %refs_9_.1) | copy-start | bytes 1572868

commit v4 on v3

--- a/solution.py
+++ b/solution.py
@@ -98,8 +98,8 @@
     core = lax.axis_index("heads")
     wk_out[...] = w[1]
     wvt_out[...] = w[2].T
-    project(both[...], wk_out[...], wvt_out[...], k_held, v_held)
     q = mm(both[pl.ds(pl.multiple_of(core * ROWS, ROWS), ROWS)], w[0]).astype(BF16).T
+    project(both[...], w[1], wvt_out[...], k_held, v_held)
     for s in range(SLOTS):
         for p in range(PAIRS):
             qs_out[s, p] = spread(q[block(p), block(s)])
@@ -134,9 +134,10 @@
 
 def far_kernel(link, partner, wk, wvt, qs, o_in, m_in, l_in, x, o_out, m_out, l_out, k_held, v_held):
     project(x[...], wk[...], wvt[...], k_held, v_held)
-    for s in range(SLOTS):
-        keys, values, _ = far_source(named_slot(partner, s, link), k_held, v_held)
-        for p in range(PAIRS):
+    slots = [named_slot(partner, s, link) for s in range(SLOTS)]
+    for p in range(PAIRS):
+        for s in range(SLOTS):
+            keys, values, _ = far_source(slots[s], k_held, v_held)
             m, l, o = merged(s, p, keys, values, qs, o_in, m_in, l_in)
             m_out[s, :, pair_block(p)] = m
             l_out[s, :, pair_block(p)] = l
@@ -149,9 +150,10 @@
 ):
     core = lax.axis_index("heads")
     project(r[pl.ds(0, ROWS)], wk[...], wvt[...], k_held, v_held)
-    for s in range(SLOTS):
-        keys, values, _ = far_source(named_slot(partner, s, link), k_held, v_held)
-        for p in range(PAIRS):
+    slots = [named_slot(partner, s, link) for s in range(SLOTS)]
+    for p in range(PAIRS):
+        for s in range(SLOTS):
+            keys, values, _ = far_source(slots[s], k_held, v_held)
             _, l, o = merged(s, p, keys, values, qs, o_in, m_in, l_in)
             share = 1.0 / l
             o = jnp.concatenate([o[i] * share[:, block(i)] for i in range(2)], axis=0)
@@ -161,19 +163,19 @@
     mean = jnp.mean(resid, axis=1, keepdims=True)
     var = jnp.mean(resid * resid, axis=1, keepdims=True) - mean * mean
     normed = (resid - mean) * lax.rsqrt(var + EPSILON)
-    hidden = jnp.maximum(mm(normed.astype(BF16), w_up[...]), 0.0).astype(BF16)
+    hidden = jnp.maximum(mm(normed.astype(BF16), w_up[...]).astype(BF16), 0.0)
     copies = []
-    for s in range(SLOTS):
-        mixed = normed[block(s)] + mm(hidden[block(s)], w_down[...])
-        done[block(s)] = jnp.where(s < counts[...], mixed, 0.0).astype(BF16)
-        copies.append(pltpu.make_async_copy(done.at[block(s)], out.at[block(s)], sems.at[s]))
-        copies[s].start()
+    for i, rows in enumerate((slice(0, 2 * BLK), slice(2 * BLK, ROWS))):
+        mixed = normed[rows] + mm(hidden[rows], w_down[...])
+        slot = lax.broadcasted_iota(jnp.int32, (mixed.shape[0], 1), 0) // BLK + 2 * i
+        done[rows] = jnp.where(slot < counts[...], mixed, 0.0).astype(BF16)
+        copies.append(pltpu.make_async_copy(done.at[rows], out.at[rows], sems.at[i]))
+        copies[i].start()
     for copy in copies:
         copy.wait()
 
 
 VMEM = pl.BlockSpec(memory_space=pltpu.VMEM)
-SMEM = pl.BlockSpec(memory_space=pltpu.SMEM)
 SPREAD = jax.ShapeDtypeStruct((SLOTS, PAIRS, BLK, 2 * BLK), BF16)
 WEIGHT = jax.ShapeDtypeStruct((D, D), BF16)
 STATE = (
@@ -185,7 +187,7 @@
 BOTH_HELD = [pltpu.VMEM((2 * ROWS, D), BF16), pltpu.VMEM((2 * SLOTS, D, BLK), BF16)]
 
 
-PAD = 400
+PAD = ROWS + 16
 
 
 def stage_kernel(x, x_out, sems):
@@ -207,7 +209,7 @@
         out_specs=VMEM,
         scratch_shapes=[pltpu.SemaphoreType.DMA((2,))],
         compiler_params=pltpu.CompilerParams(vmem_limit_bytes=4 * 2**20),
-        cost_estimate=pl.CostEstimate(flops=0, bytes_accessed=8 * 2**20, transcendentals=0),
+        cost_estimate=pl.CostEstimate(flops=0, bytes_accessed=0, transcendentals=0),
         name="stage",
     )(x)
 

time: 28.5 us -> 28.4 us (level)
  transfers between devices with their start and end apart: 3 -> 3, of which waited for: 0 -> 0; matrix products, arithmetic and copies ran while one was open for 0% -> 0% of each run, Pallas kernels for 19% -> 18%
where the time goes in v4:
time: 28.4 us; the launch traced here: 28.1 us
  starting transfers between devices  13.7 us (48%)
  Pallas kernels  9.55 us (34%)
  blocking collectives  3.72 us (13%)
  between operations  0.75 us (3%)
  local copies, waits for them, and re-layouts  0.35 us (1%)
    ppermute x3, starting transfers between devices, from_partner(): return lax.ppermute(value, axis, pairs)  13.7 us
    pallas_call x4, Pallas kernels, call(): pl.pallas_call(kernel, out_shape=outs, in_specs=[VMEM] * (len(scalars) +...  8.42 us
    all_gather x1, blocking collectives, local(): both = lax.all_gather(features, 'heads').reshape(2 * ROWS, D)  3.72 us
    pallas_call x1, Pallas kernels, stage(): pl.pallas_call(stage_kernel, out_shape=jax.ShapeDtypeStruct((PAD, D), BF1...  1.13 us
  transfers between devices with their start and end apart: 3, of which 0 were waited for; matrix products, arithmetic and copies ran while one was open for 0% of the time, Pallas kernels for 18%

profile of v4, /device:TPU:1, one launch (start us, length us, event | category | flops | bytes accessed | tf_op | source)
XLA Modules:
  0.0 28.1 jit_solution(15339356808290763325)
XLA Ops:
  0.0 0.0 copy-start
  0.0 0.0 copy-start.5
  0.0 0.0 copy-start.4
  0.0 1.1 %stage.1 = bf16[400,512]{1,0:T(8,128)(2,1)S(1)} custom-call(bf16[384,512]{1,0:T(8,128)(2,1)} %x.1), custom_call_target="tpu_custom_call" | custom-call | tf_op jit(solution)/shard_map/stage/pallas_call | solution.py:205
  1.2 5.0 %collective-permute-start.2 = (bf16[400,512]{1,0:T(8,128)(2,1)S(1)}, bf16[400,512]{1,0:T(8,128)(2,1)S(1)}, u32[]{:S(2)}, u32[]{:S(2)}) collective-permute-start(bf16[400,512]{1,0:T(8,128)(2,1)S(1)} %stage.1), channel_id=1, source_target_pairs={{0,16},{2,18},{4,20},{6,22},{8,24},{10,26},{12,28},{14,30},{16,0},... | collective-permute-start | bytes 1228808 | tf_op jit(solution)/shard_map/ppermute | solution.py:24
  6.2 4.7 %collective-permute-start = (bf16[384,512]{1,0:T(8,128)(2,1)}, bf16[384,512]{1,0:T(8,128)(2,1)S(1)}, u32[]{:S(2)}, u32[]{:S(2)}) collective-permute-start(bf16[384,512]{1,0:T(8,128)(2,1)} %x.1), channel_id=1, source_target_pairs={{0,4},{2,6},{4,0},{6,2},{8,12},{10,14},{12,8},{14,10},{16,20},{18,... | collective-permute-start | bytes 1179656 | tf_op jit(solution)/shard_map/ppermute | solution.py:24
  10.9 4.0 %collective-permute-start.1 = (bf16[384,512]{1,0:T(8,128)(2,1)}, bf16[384,512]{1,0:T(8,128)(2,1)S(1)}, u32[]{:S(2)}, u32[]{:S(2)}) collective-permute-start(bf16[384,512]{1,0:T(8,128)(2,1)} %x.1), channel_id=1, source_target_pairs={{0,64},{2,66},{4,68},{6,70},{8,72},{10,74},{12,76},{14,78},{16,80}... | collective-permute-start | bytes 1179656 | tf_op jit(solution)/shard_map/ppermute | solution.py:24
  15.5 3.7 %all-gather.both.refs_8_ = bf16[768,512]{1,0:T(8,128)(2,1)S(1)} all-gather(bf16[384,512]{1,0:T(8,128)(2,1)} %x.1), channel_id=2, replica_groups=mesh['nodes'=256,'heads'=2] {'heads'}, dimensions={0}, use_global_device_ids=true | all-gather | bytes 1179648 | tf_op jit(solution)/shard_map/all_gather | solution.py:242
  19.2 0.0 copy-done
  19.3 0.0 copy-done.5
  19.3 0.0 copy-done.4
  19.3 2.7 %own.1 = (bf16[3,4,128,256]{3,2,1,0:T(8,128)(2,1)S(1)}, bf16[512,512]{1,0:T(8,128)(2,1)S(1)}, bf16[512,512]{1,0:T(8,128)(2,1)S(1)}, f32[512,384]{1,0:T(8,128)S(1...) custom-call(s32[3,4]{1,0:T(4,128)S(1)} %copy-done.4, bf16[768,512]{1,0:T(8,128)(2,1)S(1)} %all-gather.both.refs_8_, ...), custom_call_target="tpu_custom_call" | custom-call | tf_op jit(solution)/shard_map/own/pallas_call | solution.py:218
  21.9 0.0 collective-permute-done.refs_7_
  21.9 1.3 %far.2 = (f32[512,384]{1,0:T(8,128)S(1)}, f32[3,1,1024]{2,1,0:T(1,128)S(1)}, f32[3,1,1024]{2,1,0:T(1,128)S(1)}) custom-call(s32[3,4]{1,0:T(4,128)S(1)} %copy-done.4, bf16[512,512]{1,0:T(8,128)(2,1)S(1)} %get-tuple-element.17.refs_1_.refs_2_, bf16[512,512]{1,0:T(8,128)(2,1)S(1)} %get-tuple-element.18.refs_2_.refs_3_, ...), custom_call_target="tpu_custom_call" | custom-call | tf_op jit(solution)/shard_map/far/pallas_call | solution.py:218
  23.2 0.0 copy-start.1
  23.2 0.0 copy-start.2
  23.2 0.0 copy-start.3
  23.2 0.0 collective-permute-done.1.refs_7_
  23.3 1.3 %far.3 = (f32[512,384]{1,0:T(8,128)S(1)}, f32[3,1,1024]{2,1,0:T(1,128)S(1)}, f32[3,1,1024]{2,1,0:T(1,128)S(1)}) custom-call(s32[3,4]{1,0:T(4,128)S(1)} %copy-done.4, bf16[512,512]{1,0:T(8,128)(2,1)S(1)} %get-tuple-element.17.refs_1_.refs_2_, bf16[512,512]{1,0:T(8,128)(2,1)S(1)} %get-tuple-element.18.refs_2_.refs_3_, ...), custom_call_target="tpu_custom_call" | custom-call | tf_op jit(solution)/shard_map/far/pallas_call | solution.py:218
  24.5 0.0 collective-permute-done.2.refs_12_
  24.6 0.0 copy-done.1
  24.6 0.2 copy-done.2
  24.8 0.1 copy-done.3
  24.9 3.2 %last.1 = bf16[384,512]{1,0:T(8,128)(2,1)} custom-call(s32[3,4]{1,0:T(4,128)S(1)} %copy-done.4, s32[1,1]{1,0:T(1,128)} %bitcast.3.refs_1_, bf16[512,512]{1,0:T(8,128)(2,1)S(1)} %get-tuple-element.17.refs_1_.refs_2_, bf16[512,512]{1,0:T(8,128)(2,1)S(1)} %get-tuple-element.18.refs_2_.refs_3_, bf16[3,4,128,256]{3,2,1,0:T(8,128)(2,1)S(1)} %get-tuple-element.19.refs_3_.refs_4_, ...), custom_call_target="tpu_custom_call" | custom-call | tf_op jit(solution)/shard_map/last/pallas_call | solution.py:218
Async XLA Ops:
  0.0 19.3 %copy-start = (bf16[512,3,512]{2,0,1:T(8,128)(2,1)S(1)}, bf16[512,3,512]{2,0,1:T(8,128)(2,1)}, u32[]{:S(2)}) copy-start(bf16[512,3,512]{2,0,1:T(8,128)(2,1)} %param.9) | copy-start | bytes 4718596
  0.0 19.3 %copy-start.5 = (s32[3,128,8]{1,2,0:T(8,128)S(1)}, s32[3,128,8]{1,2,0:T(8,128)}, u32[]{:S(2)}) copy-start(s32[3,128,8]{1,2,0:T(8,128)} %param.13) | copy-start | bytes 36868
  0.0 19.3 %copy-start.4 = (s32[3,4]{1,0:T(4,128)S(1)}, s32[3,4]{1,0:T(4,128)}, u32[]{:S(2)}) copy-start(s32[3,4]{1,0:T(4,128)} %refs_0_.5) | copy-start | bytes 148
  1.2 23.4 %collective-permute-start.2 = (bf16[400,512]{1,0:T(8,128)(2,1)S(1)}, bf16[400,512]{1,0:T(8,128)(2,1)S(1)}, u32[]{:S(2)}, u32[]{:S(2)}) collective-permute-start(bf16[400,512]{1,0:T(8,128)(2,1)S(1)} %stage.1), channel_id=1, source_target_pairs={{0,16},{2,18},{4,20},{6,22},{8,24},{10,26},{12,28},{14,30},{16,0},... | collective-permute-start | bytes 1228808 | tf_op jit(solution)/shard_map/ppermute | solution.py:24
  6.2 15.7 %collective-permute-start = (bf16[384,512]{1,0:T(8,128)(2,1)}, bf16[384,512]{1,0:T(8,128)(2,1)S(1)}, u32[]{:S(2)}, u32[]{:S(2)}) collective-permute-start(bf16[384,512]{1,0:T(8,128)(2,1)} %x.1), channel_id=1, source_target_pairs={{0,4},{2,6},{4,0},{6,2},{8,12},{10,14},{12,8},{14,10},{16,20},{18,... | collective-permute-start | bytes 1179656 | tf_op jit(solution)/shard_map/ppermute | solution.py:24
  10.9 12.4 %collective-permute-start.1 = (bf16[384,512]{1,0:T(8,128)(2,1)}, bf16[384,512]{1,0:T(8,128)(2,1)S(1)}, u32[]{:S(2)}, u32[]{:S(2)}) collective-permute-start(bf16[384,512]{1,0:T(8,128)(2,1)} %x.1), channel_id=1, source_target_pairs={{0,64},{2,66},{4,68},{6,70},{8,72},{10,74},{12,76},{14,78},{16,80}... | collective-permute-start | bytes 1179656 | tf_op jit(solution)/shard_map/ppermute | solution.py:24
  23.2 1.3 %copy-start.1 = (bf16[512,1024]{1,0:T(8,128)(2,1)S(1)}, bf16[512,1024]{1,0:T(8,128)(2,1)}, u32[]{:S(2)}) copy-start(bf16[512,1024]{1,0:T(8,128)(2,1)} %refs_10_.1) | copy-start | bytes 3145732
  23.2 1.5 %copy-start.2 = (bf16[1024,512]{1,0:T(8,128)(2,1)S(1)}, bf16[1024,512]{1,0:T(8,128)(2,1)}, u32[]{:S(2)}) copy-start(bf16[1024,512]{1,0:T(8,128)(2,1)} %refs_11_.1) | copy-start | bytes 3145732
  23.2 1.7 %copy-start.3 = (bf16[512,512]{1,0:T(8,128)(2,1)S(1)}, bf16[512,512]{1,0:T(8,128)(2,1)}, u32[]{:S(2)}) copy-start(bf16[512,512]{1,0:T(8,128)(2,1)} %refs_9_.1) | copy-start | bytes 1572868

commit v5 on v4

--- a/solution.py
+++ b/solution.py
@@ -187,18 +187,13 @@
 BOTH_HELD = [pltpu.VMEM((2 * ROWS, D), BF16), pltpu.VMEM((2 * SLOTS, D, BLK), BF16)]
 
 
-PAD = ROWS + 16
-
-
-def stage_kernel(x, x_out, sems):
-    copies = [
-        pltpu.make_async_copy(x, x_out.at[pl.ds(0, ROWS)], sems.at[0]),
-        pltpu.make_async_copy(x.at[pl.ds(0, PAD - ROWS)], x_out.at[pl.ds(ROWS, PAD - ROWS)], sems.at[1]),
-    ]
-    for copy in copies:
-        copy.start()
-    for copy in copies:
-        copy.wait()
+PAD = ROWS + 8
+
+
+def stage_kernel(x, x_out, sem):
+    copy = pltpu.make_async_copy(x, x_out.at[pl.ds(0, ROWS)], sem)
+    copy.start()
+    copy.wait()
 
 
 def stage(x):
@@ -207,7 +202,7 @@
         out_shape=jax.ShapeDtypeStruct((PAD, D), BF16),
         in_specs=[pl.BlockSpec(memory_space=pltpu.HBM)],
         out_specs=VMEM,
-        scratch_shapes=[pltpu.SemaphoreType.DMA((2,))],
+        scratch_shapes=[pltpu.SemaphoreType.DMA],
         compiler_params=pltpu.CompilerParams(vmem_limit_bytes=4 * 2**20),
         cost_estimate=pl.CostEstimate(flops=0, bytes_accessed=0, transcendentals=0),
         name="stage",

time: 28.4 us -> 28.4 us (level)
  no operation moved by 1% of the time
where the time goes in v5:
time: 28.4 us; the launch traced here: 28.1 us
  starting transfers between devices  13.7 us (48%)
  Pallas kernels  9.54 us (34%)
  blocking collectives  3.72 us (13%)
  between operations  0.75 us (3%)
  local copies, waits for them, and re-layouts  0.35 us (1%)
    ppermute x3, starting transfers between devices, from_partner(): return lax.ppermute(value, axis, pairs)  13.7 us
    pallas_call x4, Pallas kernels, call(): pl.pallas_call(kernel, out_shape=outs, in_specs=[VMEM] * (len(scalars) +...  8.41 us
    all_gather x1, blocking collectives, local(): both = lax.all_gather(features, 'heads').reshape(2 * ROWS, D)  3.72 us
    pallas_call x1, Pallas kernels, stage(): pl.pallas_call(stage_kernel, out_shape=jax.ShapeDtypeStruct((PAD, D), BF1...  1.12 us
  transfers between devices with their start and end apart: 3, of which 0 were waited for; matrix products, arithmetic and copies ran while one was open for 0% of the time, Pallas kernels for 18%

profile of v5, /device:TPU:1, one launch (start us, length us, event | category | flops | bytes accessed | tf_op | source)
XLA Modules:
  0.0 28.1 jit_solution(4655220267200311604)
XLA Ops:
  0.0 0.0 copy-start
  0.0 0.0 copy-start.5
  0.0 0.0 copy-start.4
  0.0 1.1 %stage.1 = bf16[392,512]{1,0:T(8,128)(2,1)S(1)} custom-call(bf16[384,512]{1,0:T(8,128)(2,1)} %x.1), custom_call_target="tpu_custom_call" | custom-call | tf_op jit(solution)/shard_map/stage/pallas_call | solution.py:200
  1.1 5.0 %collective-permute-start.2 = (bf16[392,512]{1,0:T(8,128)(2,1)S(1)}, bf16[392,512]{1,0:T(8,128)(2,1)S(1)}, u32[]{:S(2)}, u32[]{:S(2)}) collective-permute-start(bf16[392,512]{1,0:T(8,128)(2,1)S(1)} %stage.1), channel_id=1, source_target_pairs={{0,16},{2,18},{4,20},{6,22},{8,24},{10,26},{12,28},{14,30},{16,0},... | collective-permute-start | bytes 1204232 | tf_op jit(solution)/shard_map/ppermute | solution.py:24
  6.2 4.7 %collective-permute-start = (bf16[384,512]{1,0:T(8,128)(2,1)}, bf16[384,512]{1,0:T(8,128)(2,1)S(1)}, u32[]{:S(2)}, u32[]{:S(2)}) collective-permute-start(bf16[384,512]{1,0:T(8,128)(2,1)} %x.1), channel_id=1, source_target_pairs={{0,4},{2,6},{4,0},{6,2},{8,12},{10,14},{12,8},{14,10},{16,20},{18,... | collective-permute-start | bytes 1179656 | tf_op jit(solution)/shard_map/ppermute | solution.py:24
  10.9 4.0 %collective-permute-start.1 = (bf16[384,512]{1,0:T(8,128)(2,1)}, bf16[384,512]{1,0:T(8,128)(2,1)S(1)}, u32[]{:S(2)}, u32[]{:S(2)}) collective-permute-start(bf16[384,512]{1,0:T(8,128)(2,1)} %x.1), channel_id=1, source_target_pairs={{0,64},{2,66},{4,68},{6,70},{8,72},{10,74},{12,76},{14,78},{16,80}... | collective-permute-start | bytes 1179656 | tf_op jit(solution)/shard_map/ppermute | solution.py:24
  15.5 3.7 %all-gather.both.refs_8_ = bf16[768,512]{1,0:T(8,128)(2,1)S(1)} all-gather(bf16[384,512]{1,0:T(8,128)(2,1)} %x.1), channel_id=2, replica_groups=mesh['nodes'=256,'heads'=2] {'heads'}, dimensions={0}, use_global_device_ids=true | all-gather | bytes 1179648 | tf_op jit(solution)/shard_map/all_gather | solution.py:237
  19.2 0.0 copy-done
  19.2 0.0 copy-done.5
  19.2 0.0 copy-done.4
  19.2 2.7 %own.1 = (bf16[3,4,128,256]{3,2,1,0:T(8,128)(2,1)S(1)}, bf16[512,512]{1,0:T(8,128)(2,1)S(1)}, bf16[512,512]{1,0:T(8,128)(2,1)S(1)}, f32[512,384]{1,0:T(8,128)S(1...) custom-call(s32[3,4]{1,0:T(4,128)S(1)} %copy-done.4, bf16[768,512]{1,0:T(8,128)(2,1)S(1)} %all-gather.both.refs_8_, ...), custom_call_target="tpu_custom_call" | custom-call | tf_op jit(solution)/shard_map/own/pallas_call | solution.py:213
  21.9 0.0 collective-permute-done.refs_7_
  21.9 1.3 %far.2 = (f32[512,384]{1,0:T(8,128)S(1)}, f32[3,1,1024]{2,1,0:T(1,128)S(1)}, f32[3,1,1024]{2,1,0:T(1,128)S(1)}) custom-call(s32[3,4]{1,0:T(4,128)S(1)} %copy-done.4, bf16[512,512]{1,0:T(8,128)(2,1)S(1)} %get-tuple-element.17.refs_1_.refs_2_, bf16[512,512]{1,0:T(8,128)(2,1)S(1)} %get-tuple-element.18.refs_2_.refs_3_, ...), custom_call_target="tpu_custom_call" | custom-call | tf_op jit(solution)/shard_map/far/pallas_call | solution.py:213
  23.2 0.0 copy-start.1
  23.2 0.0 copy-start.2
  23.2 0.0 copy-start.3
  23.2 0.0 collective-permute-done.1.refs_7_
  23.3 1.3 %far.3 = (f32[512,384]{1,0:T(8,128)S(1)}, f32[3,1,1024]{2,1,0:T(1,128)S(1)}, f32[3,1,1024]{2,1,0:T(1,128)S(1)}) custom-call(s32[3,4]{1,0:T(4,128)S(1)} %copy-done.4, bf16[512,512]{1,0:T(8,128)(2,1)S(1)} %get-tuple-element.17.refs_1_.refs_2_, bf16[512,512]{1,0:T(8,128)(2,1)S(1)} %get-tuple-element.18.refs_2_.refs_3_, ...), custom_call_target="tpu_custom_call" | custom-call | tf_op jit(solution)/shard_map/far/pallas_call | solution.py:213
  24.5 0.0 collective-permute-done.2.refs_12_
  24.5 0.0 copy-done.1
  24.6 0.2 copy-done.2
  24.7 0.1 copy-done.3
  24.9 3.2 %last.1 = bf16[384,512]{1,0:T(8,128)(2,1)} custom-call(s32[3,4]{1,0:T(4,128)S(1)} %copy-done.4, s32[1,1]{1,0:T(1,128)} %bitcast.3.refs_1_, bf16[512,512]{1,0:T(8,128)(2,1)S(1)} %get-tuple-element.17.refs_1_.refs_2_, bf16[512,512]{1,0:T(8,128)(2,1)S(1)} %get-tuple-element.18.refs_2_.refs_3_, bf16[3,4,128,256]{3,2,1,0:T(8,128)(2,1)S(1)} %get-tuple-element.19.refs_3_.refs_4_, ...), custom_call_target="tpu_custom_call" | custom-call | tf_op jit(solution)/shard_map/last/pallas_call | solution.py:213
Async XLA Ops:
  0.0 19.2 %copy-start = (bf16[512,3,512]{2,0,1:T(8,128)(2,1)S(1)}, bf16[512,3,512]{2,0,1:T(8,128)(2,1)}, u32[]{:S(2)}) copy-start(bf16[512,3,512]{2,0,1:T(8,128)(2,1)} %param.9) | copy-start | bytes 4718596
  0.0 19.2 %copy-start.5 = (s32[3,128,8]{1,2,0:T(8,128)S(1)}, s32[3,128,8]{1,2,0:T(8,128)}, u32[]{:S(2)}) copy-start(s32[3,128,8]{1,2,0:T(8,128)} %param.13) | copy-start | bytes 36868
  0.0 19.2 %copy-start.4 = (s32[3,4]{1,0:T(4,128)S(1)}, s32[3,4]{1,0:T(4,128)}, u32[]{:S(2)}) copy-start(s32[3,4]{1,0:T(4,128)} %refs_0_.5) | copy-start | bytes 148
  1.1 23.4 %collective-permute-start.2 = (bf16[392,512]{1,0:T(8,128)(2,1)S(1)}, bf16[392,512]{1,0:T(8,128)(2,1)S(1)}, u32[]{:S(2)}, u32[]{:S(2)}) collective-permute-start(bf16[392,512]{1,0:T(8,128)(2,1)S(1)} %stage.1), channel_id=1, source_target_pairs={{0,16},{2,18},{4,20},{6,22},{8,24},{10,26},{12,28},{14,30},{16,0},... | collective-permute-start | bytes 1204232 | tf_op jit(solution)/shard_map/ppermute | solution.py:24
  6.2 15.7 %collective-permute-start = (bf16[384,512]{1,0:T(8,128)(2,1)}, bf16[384,512]{1,0:T(8,128)(2,1)S(1)}, u32[]{:S(2)}, u32[]{:S(2)}) collective-permute-start(bf16[384,512]{1,0:T(8,128)(2,1)} %x.1), channel_id=1, source_target_pairs={{0,4},{2,6},{4,0},{6,2},{8,12},{10,14},{12,8},{14,10},{16,20},{18,... | collective-permute-start | bytes 1179656 | tf_op jit(solution)/shard_map/ppermute | solution.py:24
  10.9 12.4 %collective-permute-start.1 = (bf16[384,512]{1,0:T(8,128)(2,1)}, bf16[384,512]{1,0:T(8,128)(2,1)S(1)}, u32[]{:S(2)}, u32[]{:S(2)}) collective-permute-start(bf16[384,512]{1,0:T(8,128)(2,1)} %x.1), channel_id=1, source_target_pairs={{0,64},{2,66},{4,68},{6,70},{8,72},{10,74},{12,76},{14,78},{16,80}... | collective-permute-start | bytes 1179656 | tf_op jit(solution)/shard_map/ppermute | solution.py:24
  23.2 1.3 %copy-start.1 = (bf16[512,1024]{1,0:T(8,128)(2,1)S(1)}, bf16[512,1024]{1,0:T(8,128)(2,1)}, u32[]{:S(2)}) copy-start(bf16[512,1024]{1,0:T(8,128)(2,1)} %refs_10_.1) | copy-start | bytes 3145732
  23.2 1.5 %copy-start.2 = (bf16[1024,512]{1,0:T(8,128)(2,1)S(1)}, bf16[1024,512]{1,0:T(8,128)(2,1)}, u32[]{:S(2)}) copy-start(bf16[1024,512]{1,0:T(8,128)(2,1)} %refs_11_.1) | copy-start | bytes 3145732
  23.2 1.7 %copy-start.3 = (bf16[512,512]{1,0:T(8,128)(2,1)S(1)}, bf16[512,512]{1,0:T(8,128)(2,1)}, u32[]{:S(2)}) copy-start(bf16[512,512]{1,0:T(8,128)(2,1)} %refs_9_.1) | copy-start | bytes 1572868

commit v6 on v5

--- a/solution.py
+++ b/solution.py
@@ -94,9 +94,8 @@
     return lambda p: k_held[rows, block(p)], v_held[slot], None
 
 
-def own_kernel(partner, both, w, words, qs_out, wk_out, wvt_out, o_out, m_out, l_out, k_held, v_held):
+def own_kernel(partner, both, w, words, qs_out, wvt_out, o_out, m_out, l_out, k_held, v_held):
     core = lax.axis_index("heads")
-    wk_out[...] = w[1]
     wvt_out[...] = w[2].T
     q = mm(both[pl.ds(pl.multiple_of(core * ROWS, ROWS), ROWS)], w[0]).astype(BF16).T
     project(both[...], w[1], wvt_out[...], k_held, v_held)
@@ -132,8 +131,8 @@
     return m, l, o
 
 
-def far_kernel(link, partner, wk, wvt, qs, o_in, m_in, l_in, x, o_out, m_out, l_out, k_held, v_held):
-    project(x[...], wk[...], wvt[...], k_held, v_held)
+def far_kernel(link, partner, w, wvt, qs, o_in, m_in, l_in, x, o_out, m_out, l_out, k_held, v_held):
+    project(x[...], w[1], wvt[...], k_held, v_held)
     slots = [named_slot(partner, s, link) for s in range(SLOTS)]
     for p in range(PAIRS):
         for s in range(SLOTS):
@@ -146,10 +145,10 @@
 
 
 def last_kernel(
-    link, partner, counts, wk, wvt, qs, o_in, m_in, l_in, both_x, w_out, w_up, w_down, r, out, k_held, v_held, att, done, sems,
+    link, partner, counts, w, wvt, qs, o_in, m_in, l_in, both_x, w_out, w_up, w_down, r, out, k_held, v_held, att, done, sems,
 ):
     core = lax.axis_index("heads")
-    project(r[pl.ds(0, ROWS)], wk[...], wvt[...], k_held, v_held)
+    project(r[pl.ds(0, ROWS)], w[1], wvt[...], k_held, v_held)
     slots = [named_slot(partner, s, link) for s in range(SLOTS)]
     for p in range(PAIRS):
         for s in range(SLOTS):
@@ -235,10 +234,10 @@
     for link in (1, 3):
         received[link] = exchange(features, link)
     both = lax.all_gather(features, "heads").reshape(2 * ROWS, D)
-    qs, wk, wvt, *state = call(
-        own_kernel, [partner], [both, w, words], (SPREAD, WEIGHT, WEIGHT, *STATE), BOTH_HELD, "own"
-    )
-    fixed = (wk, wvt, qs)
+    qs, wvt, *state = call(
+        own_kernel, [partner], [both, w, words], (SPREAD, WEIGHT, *STATE), BOTH_HELD, "own"
+    )
+    fixed = (w, wvt, qs)
     for link in (1, 3):
         state = call(
             lambda *refs, link=link: far_kernel(link, *refs), [partner], [*fixed, *state, received[link]], STATE, HELD, "far"

time: 28.4 us -> 28.8 us (1.014)
  the two profiles are of different devices: /device:TPU:1 before, /device:TPU:8 now
where the time goes in v6:
time: 28.8 us; the launch traced here: 28.5 us
  starting transfers between devices  13.7 us (48%)
  Pallas kernels  9.54 us (33%)
  blocking collectives  2.58 us (9%)
  waiting for transfers between devices  1.58 us (5%)
  between operations  0.73 us (3%)
  local copies, waits for them, and re-layouts  0.39 us (1%)
    ppermute x3, starting transfers between devices, from_partner(): return lax.ppermute(value, axis, pairs)  13.7 us
    pallas_call x4, Pallas kernels, call(): pl.pallas_call(kernel, out_shape=outs, in_specs=[VMEM] * (len(scalars) +...  8.42 us
    all_gather x1, blocking collectives, local(): both = lax.all_gather(features, 'heads').reshape(2 * ROWS, D)  2.58 us
    ppermute x3, waiting for transfers between devices, from_partner(): return lax.ppermute(value, axis, pairs)  1.58 us
    pallas_call x1, Pallas kernels, stage(): pl.pallas_call(stage_kernel, out_shape=jax.ShapeDtypeStruct((PAD, D), BF1...  1.12 us
  transfers between devices with their start and end apart: 3, of which 1 were waited for; matrix products, arithmetic and copies ran while one was open for 0% of the time, Pallas kernels for 18%

profile of v6, /device:TPU:8, one launch (start us, length us, event | category | flops | bytes accessed | tf_op | source)
XLA Modules:
  0.0 28.5 jit_solution(8752921057461513894)
XLA Ops:
  0.0 0.0 copy-start
  0.0 0.0 copy-start.5
  0.0 0.0 copy-start.4
  0.0 1.1 %stage.1 = bf16[392,512]{1,0:T(8,128)(2,1)S(1)} custom-call(bf16[384,512]{1,0:T(8,128)(2,1)} %x.1), custom_call_target="tpu_custom_call" | custom-call | tf_op jit(solution)/shard_map/stage/pallas_call | solution.py:199
  1.1 4.5 %collective-permute-start.2 = (bf16[392,512]{1,0:T(8,128)(2,1)S(1)}, bf16[392,512]{1,0:T(8,128)(2,1)S(1)}, u32[]{:S(2)}, u32[]{:S(2)}) collective-permute-start(bf16[392,512]{1,0:T(8,128)(2,1)S(1)} %stage.1), channel_id=1, source_target_pairs={{0,16},{2,18},{4,20},{6,22},{8,24},{10,26},{12,28},{14,30},{16,0},... | collective-permute-start | bytes 1204232 | tf_op jit(solution)/shard_map/ppermute | solution.py:24
  5.6 4.9 %collective-permute-start = (bf16[384,512]{1,0:T(8,128)(2,1)}, bf16[384,512]{1,0:T(8,128)(2,1)S(1)}, u32[]{:S(2)}, u32[]{:S(2)}) collective-permute-start(bf16[384,512]{1,0:T(8,128)(2,1)} %x.1), channel_id=1, source_target_pairs={{0,4},{2,6},{4,0},{6,2},{8,12},{10,14},{12,8},{14,10},{16,20},{18,... | collective-permute-start | bytes 1179656 | tf_op jit(solution)/shard_map/ppermute | solution.py:24
  10.6 4.3 %collective-permute-start.1 = (bf16[384,512]{1,0:T(8,128)(2,1)}, bf16[384,512]{1,0:T(8,128)(2,1)S(1)}, u32[]{:S(2)}, u32[]{:S(2)}) collective-permute-start(bf16[384,512]{1,0:T(8,128)(2,1)} %x.1), channel_id=1, source_target_pairs={{0,64},{2,66},{4,68},{6,70},{8,72},{10,74},{12,76},{14,78},{16,80}... | collective-permute-start | bytes 1179656 | tf_op jit(solution)/shard_map/ppermute | solution.py:24
  15.5 2.6 %all-gather.both.refs_8_ = bf16[768,512]{1,0:T(8,128)(2,1)S(1)} all-gather(bf16[384,512]{1,0:T(8,128)(2,1)} %x.1), channel_id=2, replica_groups=mesh['nodes'=256,'heads'=2] {'heads'}, dimensions={0}, use_global_device_ids=true | all-gather | bytes 1179648 | tf_op jit(solution)/shard_map/all_gather | solution.py:236
  18.1 0.0 copy-done
  18.1 0.0 copy-done.5
  18.1 0.0 copy-done.4
  18.1 2.7 %own.1 = (bf16[3,4,128,256]{3,2,1,0:T(8,128)(2,1)S(1)}, bf16[512,512]{1,0:T(8,128)(2,1)S(1)}, f32[512,384]{1,0:T(8,128)S(1)}, f32[3,1,1024]{2,1,0:T(1,128)S(1)}, f32[3,1,1024]{2,1,0:T(1,128)S(1)}) custom-call(s32[3,4]{1,0:T(4,128)S(1)} %copy-done.4, bf16[768,512]{1,0:T(8,128)(2,1)S(1)} %all-gather.both.refs_8_, bf16[3,512,512]{2,1,0:T(8,128)(2,1)S(1)} %bitcast.4, ...), custom_call_target="tpu_custom_call" | custom-call | tf_op jit(solution)/shard_map/own/pallas_call | solution.py:212
  20.8 0.0 collective-permute-done.refs_7_
  20.8 1.3 %far.2 = (f32[512,384]{1,0:T(8,128)S(1)}, f32[3,1,1024]{2,1,0:T(1,128)S(1)}, f32[3,1,1024]{2,1,0:T(1,128)S(1)}) custom-call(s32[3,4]{1,0:T(4,128)S(1)} %copy-done.4, bf16[3,512,512]{2,1,0:T(8,128)(2,1)S(1)} %bitcast.5, bf16[512,512]{1,0:T(8,128)(2,1)S(1)} %get-tuple-element.16.refs_2_.refs_3_, ...), custom_call_target="tpu_custom_call" | custom-call | tf_op jit(solution)/shard_map/far/pallas_call | solution.py:212
  22.1 1.6 %collective-permute-done.1.refs_7_ = bf16[384,512]{1,0:T(8,128)(2,1)S(1)} collective-permute-done((bf16[384,512]{1,0:T(8,128)(2,1)}, bf16[384,512]{1,0:T(8,128)(2,1)S(1)}, u32[]{:S(2)}, u32[]{:S(2)}) %collective-permute-start.1) | collective-permute-done | bytes 393248 | tf_op jit(solution)/shard_map/ppermute | solution.py:24
  23.6 0.0 copy-start.1
  23.6 0.0 copy-start.2
  23.6 0.0 copy-start.3
  23.6 1.3 %far.3 = (f32[512,384]{1,0:T(8,128)S(1)}, f32[3,1,1024]{2,1,0:T(1,128)S(1)}, f32[3,1,1024]{2,1,0:T(1,128)S(1)}) custom-call(s32[3,4]{1,0:T(4,128)S(1)} %copy-done.4, bf16[3,512,512]{2,1,0:T(8,128)(2,1)S(1)} %bitcast.6, bf16[512,512]{1,0:T(8,128)(2,1)S(1)} %get-tuple-element.16.refs_2_.refs_3_, ...), custom_call_target="tpu_custom_call" | custom-call | tf_op jit(solution)/shard_map/far/pallas_call | solution.py:212
  24.9 0.0 collective-permute-done.2.refs_12_
  24.9 0.0 copy-done.1
  24.9 0.2 copy-done.2
  25.2 0.1 copy-done.3
  25.3 3.2 %last.1 = bf16[384,512]{1,0:T(8,128)(2,1)} custom-call(s32[3,4]{1,0:T(4,128)S(1)} %copy-done.4, s32[1,1]{1,0:T(1,128)} %bitcast.3.refs_1_, bf16[3,512,512]{2,1,0:T(8,128)(2,1)S(1)} %bitcast.7, bf16[512,512]{1,0:T(8,128)(2,1)S(1)} %get-tuple-element.16.refs_2_.refs_3_, bf16[3,4,128,256]{3,2,1,0:T(8,128)(2,1)S(1)} %get-tuple-element.17.refs_3_.refs_4_, ...), custom_call_target="tpu_custom_call" | custom-call | tf_op jit(solution)/shard_map/last/pallas_call | solution.py:212
Async XLA Ops:
  0.0 18.1 %copy-start = (bf16[512,3,512]{2,0,1:T(8,128)(2,1)S(1)}, bf16[512,3,512]{2,0,1:T(8,128)(2,1)}, u32[]{:S(2)}) copy-start(bf16[512,3,512]{2,0,1:T(8,128)(2,1)} %param.9) | copy-start | bytes 4718596
  0.0 18.1 %copy-start.5 = (s32[3,128,8]{1,2,0:T(8,128)S(1)}, s32[3,128,8]{1,2,0:T(8,128)}, u32[]{:S(2)}) copy-start(s32[3,128,8]{1,2,0:T(8,128)} %param.13) | copy-start | bytes 36868
  0.0 18.1 %copy-start.4 = (s32[3,4]{1,0:T(4,128)S(1)}, s32[3,4]{1,0:T(4,128)}, u32[]{:S(2)}) copy-start(s32[3,4]{1,0:T(4,128)} %refs_0_.5) | copy-start | bytes 148
  1.1 23.8 %collective-permute-start.2 = (bf16[392,512]{1,0:T(8,128)(2,1)S(1)}, bf16[392,512]{1,0:T(8,128)(2,1)S(1)}, u32[]{:S(2)}, u32[]{:S(2)}) collective-permute-start(bf16[392,512]{1,0:T(8,128)(2,1)S(1)} %stage.1), channel_id=1, source_target_pairs={{0,16},{2,18},{4,20},{6,22},{8,24},{10,26},{12,28},{14,30},{16,0},... | collective-permute-start | bytes 1204232 | tf_op jit(solution)/shard_map/ppermute | solution.py:24
  5.6 15.1 %collective-permute-start = (bf16[384,512]{1,0:T(8,128)(2,1)}, bf16[384,512]{1,0:T(8,128)(2,1)S(1)}, u32[]{:S(2)}, u32[]{:S(2)}) collective-permute-start(bf16[384,512]{1,0:T(8,128)(2,1)} %x.1), channel_id=1, source_target_pairs={{0,4},{2,6},{4,0},{6,2},{8,12},{10,14},{12,8},{14,10},{16,20},{18,... | collective-permute-start | bytes 1179656 | tf_op jit(solution)/shard_map/ppermute | solution.py:24
  10.6 13.0 %collective-permute-start.1 = (bf16[384,512]{1,0:T(8,128)(2,1)}, bf16[384,512]{1,0:T(8,128)(2,1)S(1)}, u32[]{:S(2)}, u32[]{:S(2)}) collective-permute-start(bf16[384,512]{1,0:T(8,128)(2,1)} %x.1), channel_id=1, source_target_pairs={{0,64},{2,66},{4,68},{6,70},{8,72},{10,74},{12,76},{14,78},{16,80}... | collective-permute-start | bytes 1179656 | tf_op jit(solution)/shard_map/ppermute | solution.py:24
  23.6 1.3 %copy-start.1 = (bf16[512,1024]{1,0:T(8,128)(2,1)S(1)}, bf16[512,1024]{1,0:T(8,128)(2,1)}, u32[]{:S(2)}) copy-start(bf16[512,1024]{1,0:T(8,128)(2,1)} %refs_10_.1) | copy-start | bytes 3145732
  23.6 1.5 %copy-start.2 = (bf16[1024,512]{1,0:T(8,128)(2,1)S(1)}, bf16[1024,512]{1,0:T(8,128)(2,1)}, u32[]{:S(2)}) copy-start(bf16[1024,512]{1,0:T(8,128)(2,1)} %refs_11_.1) | copy-start | bytes 3145732
  23.6 1.7 %copy-start.3 = (bf16[512,512]{1,0:T(8,128)(2,1)S(1)}, bf16[512,512]{1,0:T(8,128)(2,1)}, u32[]{:S(2)}) copy-start(bf16[512,512]{1,0:T(8,128)(2,1)} %refs_9_.1) | copy-start | bytes 1572868
